TPU v7x, 32 devices: a whole 2x2x4 slice. The times are simulated.
32 devices in a mesh: row: 4 (over x, core), col: 8 (over z, y).
Axes of the slice: x: 2, y: 2, z: 4, core: 2. Of those that a mesh axis runs over, the one named last changes fastest.
Arguments:
- tokens: bfloat16 [12288, 2048], P('col', 'row'), may hold values from -6 to 6
- in_weight: float32 [2048, 6144], P(('row', 'col')), may hold values from -0.125 to 0.125
- out_weight: float32 [2048, 2048], P(('row', 'col')), may hold values from -0.125 to 0.125
- beta_weight: float32 [2048, 16], replicated, may hold values from -0.25 to 0.25
- conv_weight: float32 [4, 6144], P(None, 'row'), may hold values from -2.5 to 2.5
- conv_prior: bfloat16 [24, 3, 6144], P('col', None, 'row'), may hold values from -6 to 6
- head_gain: float32 [2048], P('row'), may hold values from 0.1 to 1.9
- state_pool: float32 [48, 16, 128, 128], P('col', 'row'), may hold values from -2.5 to 2.5
- state_index: int32 [24, 16], P('col', 'row'), may hold values from 0 to 5
- lengths: int32 [24], P('col'), may hold values from 1 to 512, 9216 in all
- page_table: int32 [24, 4, 2], P('col'), may hold values from 0 to 11, as said below
Outputs:
- server_in: bfloat16 [2048, 6144], P('row', 'col')
- server_out: bfloat16 [2048, 2048], P('row', 'col')
- layer_out: bfloat16 [12288, 2048], P('col', 'row')
- final_state: float32 [24, 16, 128, 128], P('col', 'row')
- page_cache: bfloat16 [96, 128, 2, 2048], P('col', None, None, 'row')
Inputs may be any that keep to these rules, and one draw needn't show every extreme that they name: `lengths`: one prompt has all 512 tokens live. `state_index`: which of its own index of col's 6 stored states a prompt and head continues. page_table[p, g, 0] is the index of col that keeps page g of prompt p and page_table[p, g, 1] its slot there, below 12; every slot of every index of col gets exactly one page; the prompts of one index of col send at most 3 pages to any one index of col, and exactly 3 to some.
All inputs are finite; a program needn't handle non-finite values. No bound on the sum of `lengths` on one device may be relied on, other than what follows from the above.
Results may differ from a plain program's by a relative error of at most 0.029.
Values may be sent and summed in bfloat16 or wider, within the bound.
A program may use at most 128 MiB of HBM per device.

v0:
```python
import jax
import jax.numpy as jnp
from jax import lax
from jax.sharding import PartitionSpec as P

DK = 128
STRETCH = 64
CONV = 4
SEQ = 512
PAGE = 128
PAGES_SEQ = 4


HIGHEST = lax.Precision.HIGHEST


def delta_block(carry_state, block_data):
    query_unit, key_unit, values, beta_rates = block_data
    width_c = beta_rates.shape[1]
    width_k = key_unit.shape[2]
    strict_lower = jnp.tril(jnp.ones((width_c, width_c), jnp.float32), -1)
    causal = jnp.tril(jnp.ones((width_c, width_c), jnp.float32))
    gram_matrix = jnp.einsum("bik,bjk->bij", key_unit, key_unit, precision=HIGHEST)
    system = (
        jnp.eye(width_c, dtype=jnp.float32) + beta_rates[:, :, None] * gram_matrix * strict_lower
    )
    right_side = jnp.concatenate([key_unit, values], axis=2) * beta_rates[:, :, None]
    solved = jax.scipy.linalg.solve_triangular(system, right_side, lower=True, unit_diagonal=True)
    weighted = solved[:, :, :width_k]
    corrected = solved[:, :, width_k:] - jnp.einsum(
        "bck,bkv->bcv", weighted, carry_state, precision=HIGHEST
    )
    scores = jnp.einsum("bik,bjk->bij", query_unit, key_unit, precision=HIGHEST) * causal
    output = jnp.einsum("bck,bkv->bcv", query_unit, carry_state, precision=HIGHEST) + jnp.einsum(
        "bij,bjv->biv", scores, corrected, precision=HIGHEST
    )
    carry_state = carry_state + jnp.einsum("bck,bcv->bkv", key_unit, corrected, precision=HIGHEST)
    return (carry_state, output)


def delta_scan(query_unit, key_unit, values, beta_rates, initial, block_len):
    batch_n = query_unit.shape[0]
    length_all = query_unit.shape[1]
    num_blocks = length_all // block_len

    def to_blocks(tensor):
        shaped = tensor.reshape((batch_n, num_blocks, block_len) + tensor.shape[2:])
        return jnp.moveaxis(shaped, 1, 0)

    last_state, outputs = lax.scan(
        delta_block,
        initial,
        (to_blocks(query_unit), to_blocks(key_unit), to_blocks(values), to_blocks(beta_rates)),
    )
    outputs = jnp.moveaxis(outputs, 0, 1).reshape(batch_n, length_all, -1)
    return (last_state, outputs)


def unit_rows(tensor):
    return tensor * lax.rsqrt(jnp.sum(tensor * tensor, axis=-1, keepdims=True) + 1e-06)


def local(
    tokens,
    in_weight,
    out_weight,
    beta_weight,
    conv_weight,
    conv_prior,
    head_gain,
    state_pool,
    state_index,
    lengths,
    page_table,
):
    row_count = lax.axis_size("row")
    col_count = lax.axis_size("col")
    row_id = lax.axis_index("row")
    local_tokens = tokens.shape[0]
    feature_span = tokens.shape[1]
    head_group = state_index.shape[1]
    head_width = 3 * DK
    prompts_here = lengths.shape[0]
    trainer_in = in_weight.astype(jnp.bfloat16)
    server_in, server_out = (
        lax.all_to_all(trainer_in, "col", split_axis=1, concat_axis=0, tiled=True),
        lax.all_to_all(
            out_weight.astype(jnp.bfloat16), "col", split_axis=1, concat_axis=0, tiled=True
        ),
    )
    beta_cast = beta_weight.astype(jnp.bfloat16)
    wide_in, wide_out = (
        lax.all_gather(server_in, "col", axis=1, tiled=True),
        lax.all_gather(server_out, "col", axis=1, tiled=True),
    )
    columns = wide_in
    product = jnp.dot(tokens, columns, preferred_element_type=jnp.float32)
    qkv_sum = lax.psum_scatter(
        product.reshape(local_tokens, lax.axis_size("row") * head_group, head_width)
        .transpose(1, 0, 2)
        .astype(jnp.bfloat16),
        "row",
        scatter_dimension=0,
        tiled=True,
    )
    beta_rows = lax.dynamic_slice_in_dim(beta_cast, row_id * feature_span, feature_span, 0)
    beta_term = jnp.dot(tokens, beta_rows, preferred_element_type=jnp.float32).T
    beta_sum = lax.psum_scatter(
        beta_term.astype(jnp.bfloat16), "row", scatter_dimension=0, tiled=True
    ).astype(jnp.float32)
    projected = qkv_sum.reshape(head_group, prompts_here, SEQ, head_width)
    prior_rows = conv_prior.reshape(prompts_here, CONV - 1, head_group, head_width).transpose(
        2, 0, 1, 3
    )
    padded = jnp.concatenate(
        [prior_rows.astype(jnp.float32), projected.astype(jnp.float32)], axis=2
    )
    taps_all = conv_weight.reshape(CONV, head_group, head_width)
    conv_sum = jnp.zeros(projected.shape, jnp.float32)
    for tap_id in range(CONV):
        conv_sum = (
            conv_sum + taps_all[tap_id][:, None, None, :] * padded[:, :, tap_id : tap_id + SEQ]
        )
    activated = jax.nn.silu(conv_sum).reshape(head_group * prompts_here, SEQ, 3, DK)
    query_unit = unit_rows(activated[:, :, 0])
    key_unit = unit_rows(activated[:, :, 1])
    values = activated[:, :, 2]
    live_mask = (jnp.arange(SEQ, dtype=jnp.int32)[None, :] < lengths[:, None]).astype(jnp.float32)
    live_batch = jnp.broadcast_to(live_mask[None], (head_group, prompts_here, SEQ)).reshape(
        head_group * prompts_here, SEQ
    )
    beta_rates = live_batch * jax.nn.sigmoid(beta_sum.reshape(head_group * prompts_here, SEQ))
    picked = state_pool[state_index, jnp.arange(head_group, dtype=jnp.int32)[None, :]]
    initial = picked.transpose(1, 0, 2, 3).reshape(head_group * prompts_here, DK, DK)
    last_state, outputs = delta_scan(query_unit, key_unit, values, beta_rates, initial, STRETCH)
    outputs = outputs * live_batch[:, :, None]
    normed = outputs.reshape(head_group, prompts_here, SEQ, DK)
    normed = (
        normed
        * lax.rsqrt(jnp.mean(normed * normed, axis=3, keepdims=True) + 1e-05)
        * head_gain.reshape(head_group, 1, 1, DK)
    )
    flat_heads = (
        normed.astype(jnp.bfloat16).transpose(1, 2, 0, 3).reshape(local_tokens, head_group * DK)
    )
    out_span = wide_out.shape[1] // row_count
    columns = wide_out
    product = jnp.dot(flat_heads, columns, preferred_element_type=jnp.float32)
    layer_out = (
        lax.psum_scatter(
            product.reshape(local_tokens, lax.axis_size("row") * 1, out_span)
            .transpose(1, 0, 2)
            .astype(jnp.bfloat16),
            "row",
            scatter_dimension=0,
            tiled=True,
        )
        .astype(jnp.float32)[0]
        .astype(jnp.bfloat16)
    )
    final_state = last_state.reshape(head_group, prompts_here, DK, DK).transpose(1, 0, 2, 3)
    keep_mask = live_batch[:, :, None]
    kept_pairs = jnp.stack([key_unit * keep_mask, values * keep_mask], axis=0).reshape(
        2, head_group, prompts_here, SEQ, DK
    )
    page_rows = (
        kept_pairs.transpose(2, 3, 0, 1, 4)
        .reshape(prompts_here * PAGES_SEQ, PAGE, 2, head_group * DK)
        .astype(jnp.bfloat16)
    )
    pages_dev = page_rows.shape[0]
    capacity = max(1, 2 * pages_dev // col_count)
    targets = page_table[:, :, 0].reshape(-1)
    slot_ids = page_table[:, :, 1].reshape(-1)
    order_ids = jnp.arange(pages_dev, dtype=jnp.int32)
    earlier = (targets[:, None] == targets[None, :]) & (order_ids[None, :] < order_ids[:, None])
    positions = targets * capacity + jnp.sum(earlier.astype(jnp.int32), axis=1)
    outgoing = (
        jnp.zeros((col_count * capacity,) + page_rows.shape[1:], jnp.bfloat16)
        .at[positions]
        .set(page_rows)
    )
    slot_send = jnp.full((col_count * capacity,), pages_dev, jnp.int32).at[positions].set(slot_ids)
    arrived, arrived_slots = (
        lax.all_to_all(outgoing, "col", split_axis=0, concat_axis=0, tiled=True),
        lax.all_to_all(slot_send, "col", split_axis=0, concat_axis=0, tiled=True),
    )
    page_cache = (
        jnp.zeros(page_rows.shape, jnp.bfloat16).at[arrived_slots].set(arrived, mode="drop")
    )
    return (server_in, server_out, layer_out, final_state, page_cache)


def solution(mesh):
    return jax.shard_map(
        local,
        mesh=mesh,
        in_specs=(
            P("col", "row"),
            P(("row", "col"), None),
            P(("row", "col"), None),
            P(),
            P(None, "row"),
            P("col", None, "row"),
            P("row"),
            P("col", "row", None, None),
            P("col", "row"),
            P("col"),
            P("col", None, None),
        ),
        out_specs=(
            P("row", "col"),
            P("row", "col"),
            P("col", "row"),
            P("col", "row", None, None),
            P("col", None, None, "row"),
        ),
        check_vma=False,
    )
```

profile of v0, /device:TPU:12, one launch (start us, length us, event | category | flops | bytes accessed | tf_op | source)
XLA Modules:
  0.0 1168.7 jit_solution(5418474529151111270)
XLA Ops:
  8.9 24.1 %all_to_all.55 = bf16[64,8,768]{2,0,1:T(8,128)(2,1)} all-to-all(bf16[64,8,768]{2,0,1:T(8,128)(2,1)S(1)} %bitcast.175), channel_id=1, replica_groups=mesh['row'=4,'col'=8] {'col'}, dimensions={1} | all-to-all | bytes 1572864 | tf_op jit(solution)/shard_map/all_to_all | solution.py:86
  33.2 12.9 %all_to_all.56 = bf16[64,8,256]{2,0,1:T(8,128)(2,1)} all-to-all(bf16[64,8,256]{2,0,1:T(8,128)(2,1)S(1)} %bitcast.185), channel_id=1, replica_groups=mesh['row'=4,'col'=8] {'col'}, dimensions={1} | all-to-all | bytes 524288 | tf_op jit(solution)/shard_map/all_to_all | solution.py:87
  46.2 85.9 %all-gather.3.cloned.1.call-done = bf16[512,6144]{1,0:T(8,128)(2,1)} async-done(((bf16[512,768]{1,0:T(8,128)(2,1)}), bf16[512,6144]{1,0:T(8,128)(2,1)}) %all-gather.3.cloned.1.call-update) | async-done | bytes 6291472 | tf_op jit(solution)/shard_map/all_gather | solution.py:93
  132.0 15.8 %convolution_convert_fusion = bf16[1536,6144]{1,0:T(8,128)(2,1)} fusion(bf16[1536,512]{1,0:T(8,128)(2,1)S(1)} %copy-done, bf16[512,6144]{1,0:T(8,128)(2,1)} %all-gather.3.cloned.1.call-done), kind=kOutput, calls=%fused_computation.43 | convolution fusion | flops 9673113600 | bytes 26738688 | tf_op jit(solution)/shard_map/dot_general | solution.py:97
  147.8 18.4 %copy.138 = bf16[192,16,8,384]{3,2,0,1:T(8,128)(2,1)} copy(bf16[192,16,8,384]{3,2,1,0:T(8,128)(2,1)} %bitcast.167) | data formatting | bytes 37748736 | tf_op jit(solution)/shard_map/convert_element_type | solution.py:101
  169.7 10.9 all-reduce
  187.1 138.1 %reduce-scatter.3.cloned.1.call-done = bf16[4,1536,384]{2,1,0:T(8,128)(2,1)} async-done(((bf16[16,1536,384]{2,1,0:T(8,128)(2,1)}), bf16[4,1536,384]{2,1,0:T(8,128)(2,1)}) %reduce-scatter.3.cloned.1.call-update) | async-done | bytes 4718608 | tf_op jit(solution)/shard_map/reduce_scatter | solution.py:98
  328.5 7.2 divide_multiply_fusion
  335.7 9.7 copy.99
  345.4 8.1 multiply_reduce_fusion
  370.2 554.6 %while.12 = (s32[]{:T(128)}, f32[12,128,128]{2,1,0:T(8,128)S(1)}, f32[8,12,64,128]{3,2,0,1:T(8,128)}, f32[8,12,64,128]{3,2,0,1:T(8,128)}, f32[8,12,64]{2,0,1:T(8...) while((s32[]{:T(128)}, f32[12,128,128]{2,1,0:T(8,128)S(1)}, ...), condition=%wide.region_5.6_spmd, body=%wide.region_4.5_spmd.sunk | while | flops 831590464 | bytes 12349789 | solution.py:50
  372.4 59.0 %custom-call.8 = f32[12,1,64,64]{2,3,1,0:T(8,128)S(1)} custom-call(f32[12,1,64,64]{3,2,1,0:T(8,128)S(1)} %fusion.94), custom_call_target="InvertDiagBlocksLowerTriangular" | custom-call | tf_op jit(solution)/shard_map/while/body/eval_jaxpr/jit(_solve_triangular)/vmap()/triangular_solve | solution.py:28
  441.7 59.0 %custom-call.8 = f32[12,1,64,64]{2,3,1,0:T(8,128)S(1)} custom-call(f32[12,1,64,64]{3,2,1,0:T(8,128)S(1)} %fusion.94), custom_call_target="InvertDiagBlocksLowerTriangular" | custom-call | tf_op jit(solution)/shard_map/while/body/eval_jaxpr/jit(_solve_triangular)/vmap()/triangular_solve | solution.py:28
  511.1 59.0 %custom-call.8 = f32[12,1,64,64]{2,3,1,0:T(8,128)S(1)} custom-call(f32[12,1,64,64]{3,2,1,0:T(8,128)S(1)} %fusion.94), custom_call_target="InvertDiagBlocksLowerTriangular" | custom-call | tf_op jit(solution)/shard_map/while/body/eval_jaxpr/jit(_solve_triangular)/vmap()/triangular_solve | solution.py:28
  580.4 59.0 %custom-call.8 = f32[12,1,64,64]{2,3,1,0:T(8,128)S(1)} custom-call(f32[12,1,64,64]{3,2,1,0:T(8,128)S(1)} %fusion.94), custom_call_target="InvertDiagBlocksLowerTriangular" | custom-call | tf_op jit(solution)/shard_map/while/body/eval_jaxpr/jit(_solve_triangular)/vmap()/triangular_solve | solution.py:28
  649.7 59.0 %custom-call.8 = f32[12,1,64,64]{2,3,1,0:T(8,128)S(1)} custom-call(f32[12,1,64,64]{3,2,1,0:T(8,128)S(1)} %fusion.94), custom_call_target="InvertDiagBlocksLowerTriangular" | custom-call | tf_op jit(solution)/shard_map/while/body/eval_jaxpr/jit(_solve_triangular)/vmap()/triangular_solve | solution.py:28
  719.1 59.0 %custom-call.8 = f32[12,1,64,64]{2,3,1,0:T(8,128)S(1)} custom-call(f32[12,1,64,64]{3,2,1,0:T(8,128)S(1)} %fusion.94), custom_call_target="InvertDiagBlocksLowerTriangular" | custom-call | tf_op jit(solution)/shard_map/while/body/eval_jaxpr/jit(_solve_triangular)/vmap()/triangular_solve | solution.py:28
  788.4 59.0 %custom-call.8 = f32[12,1,64,64]{2,3,1,0:T(8,128)S(1)} custom-call(f32[12,1,64,64]{3,2,1,0:T(8,128)S(1)} %fusion.94), custom_call_target="InvertDiagBlocksLowerTriangular" | custom-call | tf_op jit(solution)/shard_map/while/body/eval_jaxpr/jit(_solve_triangular)/vmap()/triangular_solve | solution.py:28
  857.7 59.0 %custom-call.8 = f32[12,1,64,64]{2,3,1,0:T(8,128)S(1)} custom-call(f32[12,1,64,64]{3,2,1,0:T(8,128)S(1)} %fusion.94), custom_call_target="InvertDiagBlocksLowerTriangular" | custom-call | tf_op jit(solution)/shard_map/while/body/eval_jaxpr/jit(_solve_triangular)/vmap()/triangular_solve | solution.py:28
  934.1 8.2 convert_bitcast_fusion
  962.0 9.9 multiply_convert_fusion.1
  988.8 8.4 scatter_fusion
  1004.9 132.7 %all-to-all-done.3 = bf16[24,128,2,512]{3,1,2,0:T(8,128)(2,1)} async-done(((bf16[24,128,2,512]{3,1,2,0:T(8,128)(2,1)}), bf16[24,128,2,512]{3,1,2,0:T(8,128)(2,1)}, u32[]{:S(2)}, u32[]{:S(2)}) %all-to-all-start.3) | async-done | bytes 6291488 | tf_op jit(solution)/shard_map/all_to_all | solution.py:185
  1139.7 14.0 %scatter_fusion.1 = bf16[12,128,2,512]{3,1,2,0:T(8,128)(2,1)} fusion(bf16[12,128,2,512]{3,1,2,0:T(8,128)(2,1)} %broadcast_in_dim.25, s32[24]{0:T(128)S(1)} %fusion.41, bf16[24,128,2,512]{3,1,2,0:T(8,128)(2,1)} %all-to-all-done.3), kind=kCustom, calls=%fused_computation.3 | custom fusion | bytes 18874464 | tf_op jit(solution)/shard_map/scatter | solution.py:189
  (225 shorter events, 176.9 us)
Async XLA Ops:
  7.2 124.8 %copy-start = (bf16[1536,512]{1,0:T(8,128)(2,1)S(1)}, bf16[1536,512]{1,0:T(8,128)(2,1)}, u32[]{:S(2)}) copy-start(bf16[1536,512]{1,0:T(8,128)(2,1)} %param.13) | copy-start | bytes 4718596
  7.2 26.0 %copy-start.5 = (f32[64,2048]{1,0:T(8,128)S(1)}, f32[64,2048]{1,0:T(8,128)}, u32[]{:S(2)}) copy-start(f32[64,2048]{1,0:T(8,128)} %param.15) | copy-start | bytes 1572868
  7.2 124.8 %all-gather.3.cloned.1.call-start = ((), (), s32[]{:S(2)}) async-start(), calls=%async_computation.6 | async-start | bytes 7077888 | tf_op jit(solution)/shard_map/all_gather | solution.py:93
  33.1 150.1 %all-gather.5.cloned.1.call-start = ((), (), s32[]{:S(2)}) async-start(), calls=%async_computation.8 | async-start | bytes 2359296 | tf_op jit(solution)/shard_map/all_gather | solution.py:94
  46.1 279.2 %reduce-scatter.3.cloned.1.call-start = ((), (), s32[]{:S(2)}) async-start(), calls=%async_computation.7 | async-start | bytes 23592960 | tf_op jit(solution)/shard_map/reduce_scatter | solution.py:98
  166.2 0.7 copy-start.7
  166.2 0.9 copy-start.6
  166.2 0.9 copy-start.12
  166.2 14.5 %copy-start.11 = (s32[3]{0:T(128)S(1)}, s32[3]{0:T(128)}, u32[]{:S(2)}) copy-start(s32[3]{0:T(128)} %param.22) | copy-start | bytes 40
  166.2 14.7 %copy-start.10 = (s32[3,4]{1,0:T(4,128)S(1)}, s32[3,4]{1,0:T(4,128)}, u32[]{:S(2)}) copy-start(s32[3,4]{1,0:T(4,128)} %param.21) | copy-start | bytes 148
  166.3 994.3 %reduce-scatter.5.cloned.1.call-start = ((), (), s32[]{:S(2)}) async-start(), calls=%async_computation.9 | async-start | bytes 7864320 | tf_op jit(solution)/shard_map/reduce_scatter | solution.py:150
  364.3 3.8 copy-start.2
  924.9 3.4 copy-start.9
  942.3 0.7 copy-start.8
  945.4 51.8 %all-to-all-start.2 = ((s32[8,3,1]{1,2,0:T(1,128)}), s32[8,3,1]{1,2,0:T(1,128)S(1)}, u32[]{:S(2)}, u32[]{:S(2)}) async-start(s32[8,3,1]{1,2,0:T(1,128)} %bitcast.41), calls=%async_computation.4 | async-start | bytes 8192 | tf_op jit(solution)/shard_map/all_to_all | solution.py:186
  997.2 140.4 %all-to-all-start.3 = ((bf16[24,128,2,512]{3,1,2,0:T(8,128)(2,1)}), bf16[24,128,2,512]{3,1,2,0:T(8,128)(2,1)}, u32[]{:S(2)}, u32[]{:S(2)}) async-start(bf16[24,128,2,512]{3,1,2,0:T(8,128)(2,1)} %scatter_fusion), calls=%async_computation.5 | async-start | bytes 12582912 | tf_op jit(solution)/shard_map/all_to_all | solution.py:185
  1139.7 22.5 %copy-start.1 = (bf16[1536,512]{1,0:T(8,128)(2,1)S(1)}, bf16[1536,512]{1,0:T(8,128)(2,1)}, u32[]{:S(2)}) copy-start(bf16[1536,512]{1,0:T(8,128)(2,1)} %param.13) | copy-start | bytes 4718596
  1153.7 6.9 copy-start.3
  1153.7 7.8 copy-start.4
Sparse Core Ops, SparseCore 0:
  33.2 98.7 all-gather.2
  134.1 48.2 all-gather.4
  184.9 140.2 reduce-scatter.2
  942.5 58.3 reduce-scatter.4
where the time goes:
time: 1180 us; the launch traced here: 1170 us
  other arithmetic  520 us (44%)
  waiting for transfers between devices  357 us (30%)
  local copies, waits for them, and re-layouts  120 us (10%)
  matrix products  96.2 us (8%)
  blocking collectives  47.9 us (4%)
  between operations  14.8 us (1%)
  starting transfers between devices  12.2 us (1%)
    another operation x32, other arithmetic, delta_block(): jax.scipy.linalg.solve_triangular(system, right_side, lower=True, unit_di...  473 us
    reduce_scatter x1, waiting for transfers between devices, local(): lax.psum_scatter(product.reshape(local_tokens, lax.axis_size('row') * hea...  138 us
    all_to_all x1, waiting for transfers between devices, local(): lax.all_to_all(outgoing, 'col', split_axis=0, concat_axis=0, tiled=True)  133 us
    all_gather x1, waiting for transfers between devices, local(): lax.all_gather(server_in, 'col', axis=1, tiled=True)  85.9 us
    all_to_all x1, blocking collectives, local(): lax.all_to_all(trainer_in, 'col', split_axis=1, concat_axis=0, tiled=True)  24.1 us
  transfers between devices with their start and end apart: 6, of which 3 were waited for; matrix products, arithmetic and copies ran while one was open for 10% of the time, Pallas kernels for 0%

commit v1 on v0

v1 whole, which is shorter than its diff:
```python
import functools

import jax
import jax.numpy as jnp
from jax import lax
from jax.experimental import pallas as pl
from jax.experimental.pallas import tpu as pltpu
from jax.sharding import PartitionSpec as P

DK = 128
CONV = 4
SEQ = 512
PAGE = 128
PAGES_SEQ = 4
BF = jnp.bfloat16
F32 = jnp.float32
VMEM_LIMIT = 48 * 1024 * 1024


def project_kernel(
    lens, spots, tok, win, wbeta, taps, prior, q_out, k_out, v_out, rates_out, outgoing, line, kv, features, weights, sems
):
    prompt, head = pl.program_id(0), pl.program_id(1)
    heads = pl.num_programs(1)
    rows = tok.shape[0]
    span = tok.shape[2]
    live = lax.broadcasted_iota(jnp.int32, (SEQ, 1), 0) < lens[prompt]

    @pl.when(head == 0)
    def _():
        for r in range(rows):
            features[:, r * span : (r + 1) * span] = tok[r]
        logits = jnp.dot(features[...], wbeta[...], preferred_element_type=F32)
        rates_out[...] = jnp.where(live, jax.nn.sigmoid(logits), 0.0)

    for r in range(rows):
        weights[r * span : (r + 1) * span, :] = win[:, r].reshape(span, 3 * DK)
    total = jnp.dot(features[...], weights[...], preferred_element_type=F32)
    line[5:8, :] = prior[0].astype(F32)
    line[8:, :] = total
    mixed = taps[0:1, :] * line[5 : 5 + SEQ, :]
    for i in range(1, CONV):
        mixed += taps[i : i + 1, :] * line[5 + i : 5 + i + SEQ, :]
    active = mixed * jax.nn.sigmoid(mixed)
    query, key, value = active[:, :DK], active[:, DK : 2 * DK], active[:, 2 * DK :]
    query = query * lax.rsqrt(jnp.sum(query * query, axis=1, keepdims=True) + 1e-06)
    key = key * lax.rsqrt(jnp.sum(key * key, axis=1, keepdims=True) + 1e-06)
    key = jnp.where(live, key, 0.0).astype(BF)
    value = jnp.where(live, value, 0.0).astype(BF)
    q_out[...] = query.astype(BF)
    k_out[...] = key
    v_out[...] = value

    def copies(p, h):
        column = pl.ds(pl.multiple_of(h * DK, DK), DK)
        return [
            pltpu.make_async_copy(
                kv.at[j, pl.ds(g * PAGE, PAGE)],
                outgoing.at[spots[p * PAGES_SEQ + g], j, :, column],
                sems.at[j, g],
            )
            for j in range(2)
            for g in range(PAGES_SEQ)
        ]

    step = prompt * heads + head

    @pl.when(step > 0)
    def _():
        for copy in copies(prompt, head):
            copy.wait()

    kv[0] = key
    kv[1] = value
    for copy in copies(prompt, head):
        copy.start()

    @pl.when(step == pl.num_programs(0) * heads - 1)
    def _():
        for copy in copies(prompt, head):
            copy.wait()


def project(tokens_all, win, wbeta, taps, prior, lengths, spots, slots):
    rows, local_tokens, span = tokens_all.shape
    cols, _, depth, width = win.shape
    heads = width // (3 * DK)
    prompts = local_tokens // SEQ
    flat = jax.ShapeDtypeStruct((local_tokens, heads * DK), BF)
    block = pl.BlockSpec((SEQ, DK), lambda p, h, *_: (p, h))
    return pl.pallas_call(
        project_kernel,
        grid_spec=pltpu.PrefetchScalarGridSpec(
            num_scalar_prefetch=2,
            grid=(prompts, heads),
            in_specs=[
                pl.BlockSpec((rows, SEQ, span), lambda p, h, *_: (0, p, 0)),
                pl.BlockSpec((cols, rows, depth, 3 * DK), lambda p, h, *_: (0, 0, 0, h)),
                pl.BlockSpec((rows * span, DK), lambda p, h, *_: (0, 0)),
                pl.BlockSpec((CONV, 3 * DK), lambda p, h, *_: (0, h)),
                pl.BlockSpec((1, CONV - 1, 3 * DK), lambda p, h, *_: (p, 0, h)),
            ],
            out_specs=[
                block,
                block,
                block,
                pl.BlockSpec((SEQ, DK), lambda p, h, *_: (p, 0)),
                pl.BlockSpec(memory_space=pl.ANY),
            ],
            scratch_shapes=[
                pltpu.VMEM((SEQ + 8, 3 * DK), F32),
                pltpu.VMEM((2, SEQ, DK), BF),
                pltpu.VMEM((SEQ, rows * span), BF),
                pltpu.VMEM((rows * span, 3 * DK), BF),
                pltpu.SemaphoreType.DMA((2, PAGES_SEQ)),
            ],
        ),
        out_shape=[
            flat,
            flat,
            flat,
            jax.ShapeDtypeStruct((local_tokens, DK), F32),
            jax.ShapeDtypeStruct((slots, 2, PAGE, heads * DK), BF),
        ],
        compiler_params=pltpu.CompilerParams(vmem_limit_bytes=VMEM_LIMIT),
        cost_estimate=pl.CostEstimate(
            flops=2 * local_tokens * rows * span * width,
            bytes_accessed=30_000_000,
            transcendentals=local_tokens * width,
        ),
        name="project",
    )(lengths, spots, tokens_all, win, wbeta, taps, prior)


def mm(a, b):
    return jnp.dot(a.astype(BF), b.astype(BF), preferred_element_type=F32)


def mm_nt(a, b):
    return lax.dot_general(a, b, (((1,), (1,)), ((), ())), preferred_element_type=F32)


def mm_tn(a, b):
    return lax.dot_general(a, b, (((0,), (0,)), ((), ())), preferred_element_type=F32)


def scan_kernel(prompt, lens, picks, q_ref, k_ref, v_ref, rates, pool, gain, normed, state_out):
    heads = pool.shape[1]
    size = PAGE
    blocks = SEQ // size
    row = lax.broadcasted_iota(jnp.int32, (size, size), 0)
    column = lax.broadcasted_iota(jnp.int32, (size, size), 1)
    lower = row > column
    causal = row >= column
    eye = (row == column).astype(F32)
    items = [(c, h) for c in range(blocks) for h in range(heads)]

    def part(ref, c, h):
        return ref[c * size : (c + 1) * size, h * DK : (h + 1) * DK]

    keys = {i: part(k_ref, *i) for i in items}
    betas = {(c, h): rates[c * size : (c + 1) * size, h : h + 1] for c, h in items}
    system = {
        i: jnp.where(lower, betas[i] * mm_nt(keys[i], keys[i]), 0.0).astype(BF) for i in items
    }
    inverse = {}
    half = 1
    while half < size:
        inside = (row // (2 * half) == column // (2 * half)) & (row // half != column // half)
        for i in items:
            corner = jnp.where(inside, system[i], jnp.zeros((), BF))
            if half == 1:
                inverse[i] = eye - corner.astype(F32)
            else:
                x = inverse[i].astype(BF)
                inverse[i] = inverse[i] - mm(x, mm(corner, x))
        half *= 2
    weighted, corrections, scores = {}, {}, {}
    for i in items:
        x = inverse[i].astype(BF)
        right = jnp.concatenate(
            [(betas[i] * keys[i].astype(F32)).astype(BF), (betas[i] * part(v_ref, *i).astype(F32)).astype(BF)],
            axis=1,
        )
        solved = mm(x, right)
        weighted[i] = solved[:, :DK].astype(BF)
        corrections[i] = solved[:, DK:]
        scores[i] = jnp.where(causal, mm_nt(part(q_ref, *i), keys[i]), 0.0).astype(BF)
    states = [pool[picks[prompt, h], h] for h in range(heads)]
    for c in range(blocks):
        live = (lax.broadcasted_iota(jnp.int32, (size, 1), 0) + c * size) < lens[prompt]
        for h in range(heads):
            i = (c, h)
            both = mm(jnp.concatenate([weighted[i], part(q_ref, *i)], axis=0), states[h])
            corrected = (corrections[i] - both[:size]).astype(BF)
            out = both[size:] + mm(scores[i], corrected)
            states[h] = states[h] + mm_tn(keys[i], corrected)
            out = jnp.where(live, out, 0.0)
            scale = lax.rsqrt(jnp.mean(out * out, axis=1, keepdims=True) + 1e-05)
            normed[c * size : (c + 1) * size, h * DK : (h + 1) * DK] = (
                out * scale * gain[:, h * DK : (h + 1) * DK]
            ).astype(BF)
    for h in range(heads):
        state_out[h] = states[h]


def scan_prompt(prompt, lengths, picks, query, key, value, rates, pool, gain):
    heads = pool.shape[1]
    wide = pl.BlockSpec((SEQ, heads * DK), lambda i, *_: (prompt, 0))
    return pl.pallas_call(
        functools.partial(scan_kernel, prompt),
        grid_spec=pltpu.PrefetchScalarGridSpec(
            num_scalar_prefetch=2,
            grid=(1,),
            in_specs=[
                wide,
                wide,
                wide,
                pl.BlockSpec((SEQ, DK), lambda i, *_: (prompt, 0)),
                pl.BlockSpec(pool.shape, lambda i, *_: (0, 0, 0, 0)),
                pl.BlockSpec((1, heads * DK), lambda i, *_: (0, 0)),
            ],
            out_specs=[
                pl.BlockSpec((SEQ, heads * DK), lambda i, *_: (0, 0)),
                pl.BlockSpec((heads, DK, DK), lambda i, *_: (0, 0, 0)),
            ],
        ),
        out_shape=[
            jax.ShapeDtypeStruct((SEQ, heads * DK), BF),
            jax.ShapeDtypeStruct((heads, DK, DK), F32),
        ],
        compiler_params=pltpu.CompilerParams(vmem_limit_bytes=VMEM_LIMIT),
        cost_estimate=pl.CostEstimate(
            flops=4_000_000_000, bytes_accessed=5_000_000, transcendentals=2048
        ),
        name="scan",
    )(lengths, picks, query, key, value, rates, pool, gain)


def out_kernel(heads_all, wout, out):
    rows, _, span = heads_all.shape
    total = jnp.zeros(out.shape, F32)
    for r in range(rows):
        total += jnp.dot(heads_all[r], wout[:, r].reshape(span, out.shape[1]), preferred_element_type=F32)
    out[...] = total.astype(BF)


def out_project(heads_all, wout):
    rows, tokens, span = heads_all.shape
    width = wout.shape[3]
    return pl.pallas_call(
        out_kernel,
        out_shape=jax.ShapeDtypeStruct((tokens, width), BF),
        compiler_params=pltpu.CompilerParams(vmem_limit_bytes=VMEM_LIMIT),
        cost_estimate=pl.CostEstimate(
            flops=2 * tokens * rows * span * width, bytes_accessed=5_000_000, transcendentals=0
        ),
        name="out_project",
    )(heads_all, wout)


def col_exchange(weight):
    rows, width = weight.shape
    cols = lax.axis_size("col")
    parts = weight.reshape(rows, cols, width // cols).transpose(1, 0, 2)
    return lax.all_to_all(parts, "col", split_axis=0, concat_axis=0, tiled=True).reshape(
        rows * cols, width // cols
    )


def local(
    tokens,
    in_weight,
    out_weight,
    beta_weight,
    conv_weight,
    conv_prior,
    head_gain,
    state_pool,
    state_index,
    lengths,
    page_table,
):
    row_count = lax.axis_size("row")
    col_count = lax.axis_size("col")
    row_id = lax.axis_index("row")
    span = tokens.shape[1]
    heads = state_index.shape[1]
    prompts = lengths.shape[0]
    depth = in_weight.shape[0]

    trainer_in = in_weight.astype(BF)
    trainer_out = out_weight.astype(BF)
    in_parts = trainer_in.reshape(depth, row_count, -1).transpose(1, 0, 2)
    out_parts = trainer_out.reshape(depth, row_count, -1).transpose(1, 0, 2)
    in_rows = lax.all_to_all(in_parts, "row", split_axis=0, concat_axis=0, tiled=True)
    win = lax.all_gather(in_rows, "col", axis=0)
    tokens_all = lax.all_gather(tokens, "row", axis=0)
    out_rows = lax.all_to_all(out_parts, "row", split_axis=0, concat_axis=0, tiled=True)
    wout = lax.all_gather(out_rows, "col", axis=0)
    server_in = col_exchange(trainer_in)
    server_out = col_exchange(trainer_out)

    my_beta = lax.dynamic_slice_in_dim(beta_weight, row_id * heads, heads, 1).astype(BF)
    wbeta = jnp.pad(my_beta, ((0, 0), (0, DK - heads)))

    pages_dev = prompts * PAGES_SEQ
    capacity = max(1, 2 * pages_dev // col_count)
    slots = capacity * col_count
    targets = page_table[:, :, 0].reshape(-1)
    slot_ids = page_table[:, :, 1].reshape(-1)
    order = jnp.arange(pages_dev, dtype=jnp.int32)
    earlier = (targets[:, None] == targets[None, :]) & (order[None, :] < order[:, None])
    spots = targets * capacity + jnp.sum(earlier.astype(jnp.int32), axis=1)
    held = spots[None, :] == jnp.arange(slots, dtype=jnp.int32)[:, None]
    slot_send = jnp.sum(jnp.where(held, slot_ids[None, :] - pages_dev, 0), axis=1) + pages_dev
    arrived_slots = lax.all_to_all(slot_send, "col", split_axis=0, concat_axis=0, tiled=True)
    sources = jnp.argmax(arrived_slots[None, :] == order[:, None], axis=1).astype(jnp.int32)

    query, key, value, rates, outgoing = project(
        tokens_all, win, wbeta, conv_weight, conv_prior, lengths, spots, slots
    )
    arrived = lax.all_to_all(outgoing, "col", split_axis=0, concat_axis=0, tiled=True)

    gain = head_gain.reshape(1, -1)
    layer_parts, state_parts = [], []
    for p in range(prompts):
        normed, state = scan_prompt(p, lengths, state_index, query, key, value, rates, state_pool, gain)
        layer_parts.append(out_project(lax.all_gather(normed, "row", axis=0), wout))
        state_parts.append(state)
    layer_out = jnp.concatenate(layer_parts, axis=0)
    final_state = jnp.stack(state_parts, axis=0)
    page_cache = jnp.take(arrived, sources, axis=0, mode="clip").transpose(0, 2, 1, 3)
    return (server_in, server_out, layer_out, final_state, page_cache)


def solution(mesh):
    return jax.shard_map(
        local,
        mesh=mesh,
        in_specs=(
            P("col", "row"),
            P(("row", "col"), None),
            P(("row", "col"), None),
            P(),
            P(None, "row"),
            P("col", None, "row"),
            P("row"),
            P("col", "row", None, None),
            P("col", "row"),
            P("col"),
            P("col", None, None),
        ),
        out_specs=(
            P("row", "col"),
            P("row", "col"),
            P("col", "row"),
            P("col", "row", None, None),
            P("col", None, None, "row"),
        ),
        check_vma=False,
    )
```

time: 1180 us -> 379 us (0.32)
  other arithmetic: 520 us -> 5.31 us
  waiting for transfers between devices: 357 us -> 215 us
  matrix products: 96.2 us -> 0 us
  local copies, waits for them, and re-layouts: 120 us -> 30 us
  Pallas kernels: 0 us -> 60.3 us
  blocking collectives: 47.9 us -> 18.3 us
  starting transfers between devices: 12.2 us -> 29.6 us
    another operation x33 -> x2, other arithmetic: 482 us -> 1.57 us  [the longest x1 0.93 us: local(): final_state = jnp.stack(state_parts, axis=0)]
    reduce_scatter x2 -> x0, waiting for transfers between devices: 138 us -> none  [the longest x1 138 us: local(): lax.psum_scatter(product.reshape(local_tokens, lax.axis_size('row') * hea...]
    all_to_all x1, waiting for transfers between devices: 133 us -> 18.4 us  [local(): lax.all_to_all(outgoing, 'col', split_axis=0, concat_axis=0, tiled=True)]
    all_gather x2 -> x6, waiting for transfers between devices: 85.9 us -> 178 us  [the longest x1 100 us: local(): win = lax.all_gather(in_rows, 'col', axis=0)]
    dot_general x51 -> x0, matrix products: 88.2 us -> none  [the longest x8 20.7 us: delta_block(): jnp.einsum('bck,bkv->bcv', query_unit, carry_state, precision=HIGHEST)]
    pallas_call x0 -> x7, Pallas kernels: none -> 60.3 us  [the longest x1 30.9 us: project(): pl.pallas_call(project_kernel, grid_spec=pltpu.PrefetchScalarGridSpec(num...]
    convert_element_type x5 -> x0, local copies, waits for them, and re-layouts: 28.1 us -> none  [the longest x1 18.4 us: local(): qkv_sum = lax.psum_scatter(product.reshape(local_tokens, lax.axis_size('r...]
    scatter x3 -> x0, local copies, waits for them, and re-layouts: 23.1 us -> none  [the longest x1 14 us: local(): jnp.zeros(page_rows.shape, jnp.bfloat16).at[arrived_slots]]
  transfers between devices with their start and end apart: 6 -> 11, of which waited for: 3 -> 9; matrix products, arithmetic and copies ran while one was open for 10% -> 3% of each run, Pallas kernels for 0% -> 16%
where the time goes in v1:
time: 379 us; the launch traced here: 373 us
  waiting for transfers between devices  215 us (57%)
  Pallas kernels  60.3 us (16%)
  local copies, waits for them, and re-layouts  30 us (8%)
  starting transfers between devices  29.6 us (8%)
  blocking collectives  18.3 us (5%)
  between operations  14.4 us (4%)
  other arithmetic  5.31 us (1%)
    all_gather x1, waiting for transfers between devices, local(): win = lax.all_gather(in_rows, 'col', axis=0)  100 us
    all_gather x3, waiting for transfers between devices, local(): layer_parts.append(out_project(lax.all_gather(normed, 'row', axis=0), wout))  68 us
    pallas_call x1, Pallas kernels, project(): pl.pallas_call(project_kernel, grid_spec=pltpu.PrefetchScalarGridSpec(num...  30.9 us
    pallas_call x3, Pallas kernels, scan_prompt(): pl.pallas_call(functools.partial(scan_kernel, prompt), grid_spec=pltpu.Pr...  25.7 us
    unnamed x46, local copies, waits for them, and re-layouts  21.6 us
    all_to_all x1, waiting for transfers between devices, local(): lax.all_to_all(outgoing, 'col', split_axis=0, concat_axis=0, tiled=True)  18.4 us
    all_to_all x1, blocking collectives, local(): lax.all_to_all(in_parts, 'row', split_axis=0, concat_axis=0, tiled=True)  18.3 us
    all_to_all x2, starting transfers between devices, col_exchange(): lax.all_to_all(parts, 'col', split_axis=0, concat_axis=0, tiled=True)  11.8 us
  transfers between devices with their start and end apart: 11, of which 9 were waited for; matrix products, arithmetic and copies ran while one was open for 3% of the time, Pallas kernels for 16%

profile of v1, /device:TPU:12, one launch (start us, length us, event | category | flops | bytes accessed | tf_op | source)
XLA Modules:
  0.0 372.6 jit_solution(5182013778403093918)
XLA Ops:
  10.2 18.3 %all_to_all.31 = bf16[4,64,1536]{2,1,0:T(8,128)(2,1)} all-to-all(bf16[4,64,1536]{2,1,0:T(8,128)(2,1)S(1)} %copy.49), channel_id=1, replica_groups=mesh['row'=4,'col'=8] {'row'}, dimensions={0} | all-to-all | bytes 1572864 | tf_op jit(solution)/shard_map/all_to_all | solution.py:296
  29.5 3.4 all-to-all-start.3
  33.2 8.8 %all-to-all-done.3 = bf16[4,64,512]{2,1,0:T(8,128)(2,1)S(1)} async-done(((bf16[4,64,512]{2,1,0:T(8,128)(2,1)}), bf16[4,64,512]{2,1,0:T(8,128)(2,1)S(1)}, u32[]{:S(2)}, u32[]{:S(2)}) %all-to-all-start.3) | async-done | bytes 262176 | tf_op jit(solution)/shard_map/all_to_all | solution.py:299
  43.7 6.4 %all-to-all-start.5 = ((s32[8,3,1]{1,2,0:T(1,128)}), s32[8,3,1]{1,2,0:T(1,128)S(1)}, u32[]{:S(2)}, u32[]{:S(2)}) async-start(s32[8,3,1]{1,2,0:T(1,128)} %bitcast.16), calls=%async_computation.5 | async-start | bytes 8192 | tf_op jit(solution)/shard_map/all_to_all | solution.py:317
  50.9 3.3 all-to-all-done.5
  54.2 5.7 %all-to-all-start.1 = ((bf16[8,64,256]{2,1,0:T(8,128)(2,1)}), bf16[8,64,256]{2,1,0:T(8,128)(2,1)S(1)}, u32[]{:S(2)}, u32[]{:S(2)}) async-start(bf16[8,64,256]{2,1,0:T(8,128)(2,1)} %bitcast.30), calls=%async_computation.1 | async-start | bytes 524288 | tf_op jit(solution)/shard_map/all_to_all | solution.py:266
  60.8 5.3 %all-to-all-done.1 = bf16[8,64,256]{2,1,0:T(8,128)(2,1)S(1)} async-done(((bf16[8,64,256]{2,1,0:T(8,128)(2,1)}), bf16[8,64,256]{2,1,0:T(8,128)(2,1)S(1)}, u32[]{:S(2)}, u32[]{:S(2)}) %all-to-all-start.1) | async-done | bytes 262176 | tf_op jit(solution)/shard_map/all_to_all | solution.py:266
  66.1 6.1 %all-to-all-start = ((bf16[8,64,768]{2,1,0:T(8,128)(2,1)}), bf16[8,64,768]{2,1,0:T(8,128)(2,1)}, u32[]{:S(2)}, u32[]{:S(2)}) async-start(bf16[8,64,768]{2,1,0:T(8,128)(2,1)} %bitcast.28), calls=%async_computation | async-start | bytes 1572864 | tf_op jit(solution)/shard_map/all_to_all | solution.py:266
  72.7 100.3 %all-gather.15.cloned.1.call-done = bf16[32,64,1536]{2,1,0:T(8,128)(2,1)} async-done(((bf16[4,64,1536]{2,1,0:T(8,128)(2,1)}), bf16[32,64,1536]{2,1,0:T(8,128)(2,1)}) %all-gather.15.cloned.1.call-update) | async-done | bytes 6291472 | tf_op jit(solution)/shard_map/all_gather | solution.py:297
  173.1 30.9 %project.1 = (bf16[1536,512]{1,0:T(8,128)(2,1)S(1)}, bf16[1536,512]{1,0:T(8,128)(2,1)S(1)}, bf16[1536,512]{1,0:T(8,128)(2,1)S(1)}, f32[1536,128]{1,0:T(8,128)S(1)}, bf16[24,2,128,512]{3,2,1,0:T(8,128)(2,1)}) custom-call(s32[3]{0:T(128)S(1)} %copy-done.10, s32[12]{0:T(128)S(1)} %multiply_add_fusion.spots, bf16[4,1536,512]{2,1,0:T(8,128)(2,1)} %bitcast.49, ...), custom_call_target="tpu_custom_call" | custom-call | flops 9663676416 | bytes 30000000 | tf_op jit(solution)/shard_map/project/pallas_call | solution.py:91
  206.3 7.6 %all-to-all-start.4 = ((bf16[24,2,128,512]{3,2,1,0:T(8,128)(2,1)}), bf16[24,2,128,512]{3,2,1,0:T(8,128)(2,1)}, u32[]{:S(2)}, u32[]{:S(2)}) async-start(bf16[24,2,128,512]{3,2,1,0:T(8,128)(2,1)} %get-tuple-element.27), calls=%async_computation.4 | async-start | bytes 12582912 | tf_op jit(solution)/shard_map/all_to_all | solution.py:323
  215.3 8.5 %scan.3 = (bf16[512,512]{1,0:T(8,128)(2,1)}, f32[4,128,128]{2,1,0:T(8,128)S(1)}) custom-call(s32[3]{0:T(128)S(1)} %copy-done.10, s32[3,4]{1,0:T(4,128)S(1)} %copy-done.8, bf16[1536,512]{1,0:T(8,128)(2,1)S(1)} %get-tuple-element.17.q_ref, bf16[1536,512]{1,0:T(8,128)(2,1)S(1)} %copy-done.12, bf16[1536,512]{1,0:T(8,128)(2,1)} %copy-done.15, ...), custom_call_target="tpu_custom_call" | custom-call | flops 4000000000 | bytes 5000000 | tf_op jit(solution)/shard_map/scan/pallas_call | solution.py:210
  225.5 8.6 %scan.4 = (bf16[512,512]{1,0:T(8,128)(2,1)}, f32[4,128,128]{2,1,0:T(8,128)S(1)}) custom-call(s32[3]{0:T(128)S(1)} %copy-done.10, s32[3,4]{1,0:T(4,128)S(1)} %copy-done.8, bf16[1536,512]{1,0:T(8,128)(2,1)S(1)} %get-tuple-element.17.q_ref, bf16[1536,512]{1,0:T(8,128)(2,1)S(1)} %copy-done.13, bf16[1536,512]{1,0:T(8,128)(2,1)} %copy-done.15, ...), custom_call_target="tpu_custom_call" | custom-call | flops 4000000000 | bytes 5000000 | tf_op jit(solution)/shard_map/scan/pallas_call | solution.py:210
  235.6 8.5 %scan.5 = (bf16[512,512]{1,0:T(8,128)(2,1)}, f32[4,128,128]{2,1,0:T(8,128)S(1)}) custom-call(s32[3]{0:T(128)S(1)} %copy-done.10, s32[3,4]{1,0:T(4,128)S(1)} %copy-done.8, bf16[1536,512]{1,0:T(8,128)(2,1)S(1)} %get-tuple-element.17.q_ref, bf16[1536,512]{1,0:T(8,128)(2,1)S(1)} %copy-done.14, bf16[1536,512]{1,0:T(8,128)(2,1)} %copy-done.15, ...), custom_call_target="tpu_custom_call" | custom-call | flops 4000000000 | bytes 5000000 | tf_op jit(solution)/shard_map/scan/pallas_call | solution.py:210
  247.0 9.9 %all-gather.19.cloned.1.call-done = bf16[32,64,512]{2,1,0:T(8,128)(2,1)} async-done(((bf16[4,64,512]{2,1,0:T(8,128)(2,1)}), bf16[32,64,512]{2,1,0:T(8,128)(2,1)}) %all-gather.19.cloned.1.call-update) | async-done | bytes 2097168 | tf_op jit(solution)/shard_map/all_gather | solution.py:300
  256.9 26.6 %all-gather.17.cloned.1.call-done = bf16[2048,512]{1,0:T(8,128)(2,1)} async-done(((bf16[512,512]{1,0:T(8,128)(2,1)}), bf16[2048,512]{1,0:T(8,128)(2,1)}) %all-gather.17.cloned.1.call-update) | async-done | bytes 2097168 | tf_op jit(solution)/shard_map/all_gather | solution.py:329
  283.4 1.6 copy-done.1
  287.9 19.6 %all-gather.21.cloned.1.call-done = bf16[2048,512]{1,0:T(8,128)(2,1)} async-done(((bf16[512,512]{1,0:T(8,128)(2,1)}), bf16[2048,512]{1,0:T(8,128)(2,1)}) %all-gather.21.cloned.1.call-update) | async-done | bytes 2097168 | tf_op jit(solution)/shard_map/all_gather | solution.py:329
  307.5 1.6 copy-done.4
  310.3 21.8 %all-gather.23.cloned.1.call-done = bf16[2048,512]{1,0:T(8,128)(2,1)} async-done(((bf16[512,512]{1,0:T(8,128)(2,1)}), bf16[2048,512]{1,0:T(8,128)(2,1)}) %all-gather.23.cloned.1.call-update) | async-done | bytes 2097168 | tf_op jit(solution)/shard_map/all_gather | solution.py:329
  336.2 18.4 %all-to-all-done.4 = bf16[24,2,128,512]{3,2,1,0:T(8,128)(2,1)} async-done(((bf16[24,2,128,512]{3,2,1,0:T(8,128)(2,1)}), bf16[24,2,128,512]{3,2,1,0:T(8,128)(2,1)}, u32[]{:S(2)}, u32[]{:S(2)}) %all-to-all-start.4) | async-done | bytes 6291488 | tf_op jit(solution)/shard_map/all_to_all | solution.py:323
  354.6 3.5 gather_fusion
  358.1 4.9 %copy.53 = bf16[12,128,2,512]{3,2,1,0:T(2,128)(2,1)} copy(bf16[12,128,2,512]{3,1,2,0:T(8,128)(2,1)S(1)} %bitcast.43) | data formatting | bytes 6291456
  363.0 2.1 copy.63
  (84 shorter events, 26.5 us)
Async XLA Ops:
  7.2 65.1 %copy-start = (f32[2048,16]{0,1:T(8,128)S(1)}, f32[2048,16]{0,1:T(8,128)}, u32[]{:S(2)}) copy-start(f32[2048,16]{0,1:T(8,128)} %param.14) | copy-start | bytes 393220
  7.2 65.6 %all-gather.13.cloned.1.call-start = ((), (), s32[]{:S(2)}) async-start(), calls=%async_computation.6 | async-start | bytes 7864320 | tf_op jit(solution)/shard_map/all_gather | solution.py:298
  7.9 165.2 %all-gather.15.cloned.1.call-start = ((), (), s32[]{:S(2)}) async-start(), calls=%async_computation.7 | async-start | bytes 7077888 | tf_op jit(solution)/shard_map/all_gather | solution.py:297
  9.5 19.1 %copy-start.19 = (f32[64,2048]{1,0:T(8,128)S(1)}, f32[64,2048]{1,0:T(8,128)}, u32[]{:S(2)}) copy-start(f32[64,2048]{1,0:T(8,128)} %param.13) | copy-start | bytes 1572868
  10.0 23.0 %copy-start.20 = (s32[3,4,2]{1,2,0:T(2,128)S(1)}, s32[3,4,2]{1,2,0:T(2,128)}, u32[]{:S(2)}) copy-start(s32[3,4,2]{1,2,0:T(2,128)} %param.21) | copy-start | bytes 292
  29.5 12.5 %all-to-all-start.3 = ((bf16[4,64,512]{2,1,0:T(8,128)(2,1)}), bf16[4,64,512]{2,1,0:T(8,128)(2,1)S(1)}, u32[]{:S(2)}, u32[]{:S(2)}) async-start(bf16[4,64,512]{2,1,0:T(8,128)(2,1)} %copy.51), calls=%async_computation.3 | async-start | bytes 524288 | tf_op jit(solution)/shard_map/all_to_all | solution.py:299
  32.9 140.2 %copy-start.6 = (bf16[3,3,1536]{2,1,0:T(4,128)(2,1)S(1)}, bf16[3,3,1536]{2,1,0:T(4,128)(2,1)}, u32[]{:S(2)}) copy-start(bf16[3,3,1536]{2,1,0:T(4,128)(2,1)} %prior.1) | copy-start | bytes 82948
  32.9 140.2 %copy-start.7 = (f32[4,1536]{1,0:T(4,128)S(1)}, f32[4,1536]{1,0:T(4,128)}, u32[]{:S(2)}) copy-start(f32[4,1536]{1,0:T(4,128)} %taps.1) | copy-start | bytes 73732
  32.9 140.1 %copy-start.10 = (s32[3]{0:T(128)S(1)}, s32[3]{0:T(128)}, u32[]{:S(2)}) copy-start(s32[3]{0:T(128)} %lens.7) | copy-start | bytes 40
  33.0 223.9 %all-gather.19.cloned.1.call-start = ((), (), s32[]{:S(2)}) async-start(), calls=%async_computation.9 | async-start | bytes 2359296 | tf_op jit(solution)/shard_map/all_gather | solution.py:300
  43.7 10.4 %all-to-all-start.5 = ((s32[8,3,1]{1,2,0:T(1,128)}), s32[8,3,1]{1,2,0:T(1,128)S(1)}, u32[]{:S(2)}, u32[]{:S(2)}) async-start(s32[8,3,1]{1,2,0:T(1,128)} %bitcast.16), calls=%async_computation.5 | async-start | bytes 8192 | tf_op jit(solution)/shard_map/all_to_all | solution.py:317
  54.2 11.9 %all-to-all-start.1 = ((bf16[8,64,256]{2,1,0:T(8,128)(2,1)}), bf16[8,64,256]{2,1,0:T(8,128)(2,1)S(1)}, u32[]{:S(2)}, u32[]{:S(2)}) async-start(bf16[8,64,256]{2,1,0:T(8,128)(2,1)} %bitcast.30), calls=%async_computation.1 | async-start | bytes 524288 | tf_op jit(solution)/shard_map/all_to_all | solution.py:266
  66.1 6.1 %copy-start.17 = (bf16[8,64,256]{2,1,0:T(8,128)(2,1)}, bf16[8,64,256]{2,1,0:T(8,128)(2,1)S(1)}, u32[]{:S(2)}) copy-start(bf16[8,64,256]{2,1,0:T(8,128)(2,1)S(1)} %all-to-all-done.1) | copy-start | bytes 786436
  66.1 140.2 %all-to-all-start = ((bf16[8,64,768]{2,1,0:T(8,128)(2,1)}), bf16[8,64,768]{2,1,0:T(8,128)(2,1)}, u32[]{:S(2)}, u32[]{:S(2)}) async-start(bf16[8,64,768]{2,1,0:T(8,128)(2,1)} %bitcast.28), calls=%async_computation | async-start | bytes 1572864 | tf_op jit(solution)/shard_map/all_to_all | solution.py:266
  206.3 7.6 %copy-start.8 = (s32[3,4]{1,0:T(4,128)S(1)}, s32[3,4]{1,0:T(4,128)}, u32[]{:S(2)}) copy-start(s32[3,4]{1,0:T(4,128)} %picks.5) | copy-start | bytes 148
  206.3 7.6 %copy-start.9 = (f32[512]{0:T(512)S(1)}, f32[512]{0:T(512)}, u32[]{:S(2)}) copy-start(f32[512]{0:T(512)} %param.17) | copy-start | bytes 6148
  206.3 148.3 %all-to-all-start.4 = ((bf16[24,2,128,512]{3,2,1,0:T(8,128)(2,1)}), bf16[24,2,128,512]{3,2,1,0:T(8,128)(2,1)}, u32[]{:S(2)}, u32[]{:S(2)}) async-start(bf16[24,2,128,512]{3,2,1,0:T(8,128)(2,1)} %get-tuple-element.27), calls=%async_computation.4 | async-start | bytes 12582912 | tf_op jit(solution)/shard_map/all_to_all | solution.py:323
  213.9 69.6 %all-gather.17.cloned.1.call-start = ((), (), s32[]{:S(2)}) async-start(), calls=%async_computation.8 | async-start | bytes 2621440 | tf_op jit(solution)/shard_map/all_gather | solution.py:329
  223.9 83.6 %all-gather.21.cloned.1.call-start = ((), (), s32[]{:S(2)}) async-start(), calls=%async_computation.10 | async-start | bytes 2621440 | tf_op jit(solution)/shard_map/all_gather | solution.py:329
  234.1 98.0 %all-gather.23.cloned.1.call-start = ((), (), s32[]{:S(2)}) async-start(), calls=%async_computation.11 | async-start | bytes 2621440 | tf_op jit(solution)/shard_map/all_gather | solution.py:329
  283.4 1.6 copy-start.1
  286.6 20.8 %copy-start.2 = (bf16[32,64,512]{2,1,0:T(8,128)(2,1)S(1)}, bf16[32,64,512]{2,1,0:T(8,128)(2,1)}, u32[]{:S(2)}) copy-start(bf16[32,64,512]{2,1,0:T(8,128)(2,1)} %all-gather.19.cloned.1.call-done) | copy-start | bytes 6291460
  307.5 1.6 copy-start.4
  358.1 7.0 %copy-start.18 = (bf16[8,64,256]{2,1,0:T(8,128)(2,1)S(1)}, bf16[8,64,256]{2,1,0:T(8,128)(2,1)}, u32[]{:S(2)}) copy-start(bf16[8,64,256]{2,1,0:T(8,128)(2,1)} %copy-done.17) | copy-start | bytes 786436
  (8 other events, 10.4 us)
Sparse Core Ops, SparseCore 0:
  9.6 53.4 all-gather.12
  65.3 107.7 all-gather.14
  175.2 81.6 all-gather.18
  258.3 25.1 all-gather.16
  284.9 22.5 all-gather.20
  309.5 22.5 all-gather.22

commit v2 on v1

--- a/solution.py
+++ b/solution.py
@@ -15,6 +15,175 @@
 BF = jnp.bfloat16
 F32 = jnp.float32
 VMEM_LIMIT = 48 * 1024 * 1024
+
+
+MESH = pl.DeviceIdType.MESH
+
+
+def handover_kernel(
+    chain, in_parts, out_parts, tokens, win, out_rows, tokens_all, own, part_send, part_recv, tok_send, tok_recv,
+    chain_send, chain_recv, pair_send, pair_recv,
+):
+    row, col = lax.axis_index("row"), lax.axis_index("col")
+    rows = in_parts.shape[0]
+    place, side = col // 2, col % 2
+    twin = row + 1 - 2 * (row % 2)
+    across = lax.rem(row + 2, rows)
+    partner = col + 1 - 2 * side
+    chunks = tok_send.shape[1]
+    span = tokens.shape[0] // chunks
+
+    barrier = pltpu.get_barrier_semaphore()
+    for d in range(1, rows):
+        pl.semaphore_signal(barrier, inc=1, device_id=(lax.rem(row + d, rows), col), device_id_type=MESH)
+    pl.semaphore_signal(barrier, inc=1, device_id=(row, partner), device_id_type=MESH)
+
+    @pl.when(place > 0)
+    def _():
+        pl.semaphore_signal(barrier, inc=1, device_id=(row, col - 2), device_id_type=MESH)
+
+    @pl.when(place < chain - 1)
+    def _():
+        pl.semaphore_signal(barrier, inc=1, device_id=(row, col + 2), device_id_type=MESH)
+
+    neighbours = lax.div(place + chain - 1, chain) + lax.div(2 * (chain - 1) - place, chain)
+    pl.semaphore_wait(barrier, rows + neighbours)
+
+    def remote(src, dst, send, recv, target):
+        return pltpu.make_async_remote_copy(
+            src_ref=src, dst_ref=dst, send_sem=send, recv_sem=recv, device_id=target, device_id_type=MESH
+        )
+
+    part_copies = []
+    for d in range(1, rows):
+        peer = lax.rem(row + d, rows)
+        part_copies.append(
+            remote(in_parts.at[peer], win.at[col, row], part_send.at[0, d], part_recv.at[0, d], (peer, col))
+        )
+        part_copies.append(
+            remote(out_parts.at[peer], out_rows.at[row], part_send.at[1, d], part_recv.at[1, d], (peer, col))
+        )
+    for copy in part_copies:
+        copy.start()
+    own_copies = [
+        pltpu.make_async_copy(in_parts.at[row], win.at[col, row], own.at[0]),
+        pltpu.make_async_copy(out_parts.at[row], out_rows.at[row], own.at[1]),
+        pltpu.make_async_copy(tokens, tokens_all.at[row], own.at[2]),
+    ]
+    for copy in own_copies:
+        copy.start()
+
+    def chunk(slot, n):
+        return tokens_all.at[slot, pl.ds(n * span, span)]
+
+    def token_copy(kind, n):
+        mine = tokens.at[pl.ds(n * span, span)]
+        src = chunk(across, n) if kind == 2 else mine
+        dst = chunk(across if kind == 2 else row, n)
+        target = (across, col) if kind == 0 else (twin, col)
+        return remote(src, dst, tok_send.at[kind, n], tok_recv.at[kind, n], target)
+
+    for n in range(chunks):
+        token_copy(0, n).start()
+    for n in range(chunks):
+        token_copy(1, n).start()
+
+    def chain_copy(way, s):
+        block = col - 2 * s if way == 0 else col + 2 * s
+        target = (row, col + 2) if way == 0 else (row, col - 2)
+        return remote(
+            win.at[block], win.at[block], chain_send.at[way, s], chain_recv.at[way, s], target
+        )
+
+    def pair_copy(way, s):
+        block = col - 2 * s if way == 0 else col + 2 * s
+        return remote(win.at[block], win.at[block], pair_send.at[way, s], pair_recv.at[way, s], (row, partner))
+
+    def held(way, s):
+        return place - s >= 0 if way == 0 else place + s < chain
+
+    def goes_on(way):
+        return place < chain - 1 if way == 0 else place > 0
+
+    own_copies[0].wait()
+    for d in range(1, rows):
+        part_copies[2 * (d - 1)].wait_recv()
+    for s in range(chain):
+        for way in range(2):
+
+            @pl.when(held(way, s))
+            def _():
+                if s > 0:
+                    chain_copy(way, s - 1).wait_recv()
+
+                @pl.when(goes_on(way))
+                def _():
+                    chain_copy(way, s).start()
+
+                if s > 0 or way == 0:
+                    pair_copy(way, s).start()
+
+        if 0 < s <= chunks:
+            token_copy(0, s - 1).wait_recv()
+            token_copy(2, s - 1).start()
+    for n in range(max(0, chain - 1), chunks):
+        token_copy(0, n).wait_recv()
+        token_copy(2, n).start()
+    for n in range(chunks):
+        token_copy(1, n).wait_recv()
+        token_copy(2, n).wait_recv()
+        for kind in range(3):
+            token_copy(kind, n).wait_send()
+    for d in range(1, rows):
+        part_copies[2 * (d - 1)].wait_send()
+        part_copies[2 * (d - 1) + 1].wait()
+    own_copies[1].wait()
+    own_copies[2].wait()
+    for s in range(chain):
+        for way in range(2):
+
+            @pl.when(held(way, s))
+            def _():
+                @pl.when(goes_on(way))
+                def _():
+                    chain_copy(way, s).wait_send()
+
+                if s > 0 or way == 0:
+                    pair_copy(way, s).wait()
+
+
+def handover(in_parts, out_parts, tokens, cols):
+    rows, depth, width = in_parts.shape
+    chain = cols // 2
+    chunks = tokens.shape[0] // SEQ
+    dma = pltpu.SemaphoreType.DMA
+    anywhere = pl.BlockSpec(memory_space=pl.ANY)
+    return pl.pallas_call(
+        functools.partial(handover_kernel, chain),
+        in_specs=[anywhere] * 3,
+        out_specs=[anywhere] * 3,
+        out_shape=[
+            jax.ShapeDtypeStruct((cols, rows, depth, width), BF),
+            jax.ShapeDtypeStruct(out_parts.shape, BF),
+            jax.ShapeDtypeStruct((rows,) + tokens.shape, BF),
+        ],
+        scratch_shapes=[
+            dma((3,)),
+            dma((2, rows)),
+            dma((2, rows)),
+            dma((3, chunks)),
+            dma((3, chunks)),
+            dma((2, chain)),
+            dma((2, chain)),
+            dma((2, chain)),
+            dma((2, chain)),
+        ],
+        compiler_params=pltpu.CompilerParams(
+            collective_id=0, has_side_effects=True, vmem_limit_bytes=VMEM_LIMIT
+        ),
+        cost_estimate=pl.CostEstimate(flops=0, bytes_accessed=300_000_000, transcendentals=0),
+        name="handover",
+    )(in_parts, out_parts, tokens)
 
 
 def project_kernel(
@@ -293,13 +462,8 @@
     trainer_out = out_weight.astype(BF)
     in_parts = trainer_in.reshape(depth, row_count, -1).transpose(1, 0, 2)
     out_parts = trainer_out.reshape(depth, row_count, -1).transpose(1, 0, 2)
-    in_rows = lax.all_to_all(in_parts, "row", split_axis=0, concat_axis=0, tiled=True)
-    win = lax.all_gather(in_rows, "col", axis=0)
-    tokens_all = lax.all_gather(tokens, "row", axis=0)
-    out_rows = lax.all_to_all(out_parts, "row", split_axis=0, concat_axis=0, tiled=True)
+    win, out_rows, tokens_all = handover(in_parts, out_parts, tokens, col_count)
     wout = lax.all_gather(out_rows, "col", axis=0)
-    server_in = col_exchange(trainer_in)
-    server_out = col_exchange(trainer_out)
 
     my_beta = lax.dynamic_slice_in_dim(beta_weight, row_id * heads, heads, 1).astype(BF)
     wbeta = jnp.pad(my_beta, ((0, 0), (0, DK - heads)))
@@ -320,6 +484,9 @@
     query, key, value, rates, outgoing = project(
         tokens_all, win, wbeta, conv_weight, conv_prior, lengths, spots, slots
     )
+    trainer_in, trainer_out, rates = lax.optimization_barrier((trainer_in, trainer_out, rates))
+    server_in = col_exchange(trainer_in)
+    server_out = col_exchange(trainer_out)
     arrived = lax.all_to_all(outgoing, "col", split_axis=0, concat_axis=0, tiled=True)
 
     gain = head_gain.reshape(1, -1)

time: 379 us -> 397 us (1.047)
  Pallas kernels: 60.3 us -> 137 us
  waiting for transfers between devices: 215 us -> 162 us
  starting transfers between devices: 29.6 us -> 22 us
  blocking collectives: 18.3 us -> 23.2 us
    all_gather x1, waiting for transfers between devices: 9.89 us -> 111 us  [local(): wout = lax.all_gather(out_rows, 'col', axis=0)]
    all_gather x2 -> x0, waiting for transfers between devices: 100 us -> none  [the longest x1 100 us: local(): win = lax.all_gather(in_rows, 'col', axis=0)]
    pallas_call x0 -> x1, Pallas kernels: none -> 76.7 us  [handover(): pl.pallas_call(functools.partial(handover_kernel, chain), in_specs=[anywh...]
    all_gather x3, waiting for transfers between devices: 68 us -> 41.7 us  [local(): layer_parts.append(out_project(lax.all_gather(normed, 'row', axis=0), wout))]
    all_to_all x1, waiting for transfers between devices: 18.4 us -> 0.01 us  [local(): lax.all_to_all(outgoing, 'col', split_axis=0, concat_axis=0, tiled=True)]
    all_to_all x1 -> x0, waiting for transfers between devices: 8.85 us -> none  [local(): lax.all_to_all(out_parts, 'row', split_axis=0, concat_axis=0, tiled=True)]
    all_to_all x2 -> x1, starting transfers between devices: 11.8 us -> 6.28 us  [col_exchange(): lax.all_to_all(parts, 'col', split_axis=0, concat_axis=0, tiled=True)]
    all_to_all x1, blocking collectives: 18.3 us -> 23.2 us  [col_exchange(): lax.all_to_all(parts, 'col', split_axis=0, concat_axis=0, tiled=True)]
  transfers between devices with their start and end apart: 11 -> 7, of which waited for: 9 -> 5; matrix products, arithmetic and copies ran while one was open for 3% -> 2% of each run, Pallas kernels for 16% -> 5%
where the time goes in v2:
time: 397 us; the launch traced here: 394 us
  waiting for transfers between devices  162 us (41%)
  Pallas kernels  137 us (35%)
  local copies, waits for them, and re-layouts  28.7 us (7%)
  blocking collectives  23.2 us (6%)
  starting transfers between devices  22 us (6%)
  between operations  14 us (4%)
  other arithmetic  7.42 us (2%)
    all_gather x1, waiting for transfers between devices, local(): wout = lax.all_gather(out_rows, 'col', axis=0)  111 us
    pallas_call x1, Pallas kernels, handover(): pl.pallas_call(functools.partial(handover_kernel, chain), in_specs=[anywh...  76.7 us
    all_gather x3, waiting for transfers between devices, local(): layer_parts.append(out_project(lax.all_gather(normed, 'row', axis=0), wout))  41.7 us
    pallas_call x1, Pallas kernels, project(): pl.pallas_call(project_kernel, grid_spec=pltpu.PrefetchScalarGridSpec(num...  30.8 us
    pallas_call x3, Pallas kernels, scan_prompt(): pl.pallas_call(functools.partial(scan_kernel, prompt), grid_spec=pltpu.Pr...  25.6 us
    all_to_all x1, blocking collectives, col_exchange(): lax.all_to_all(parts, 'col', split_axis=0, concat_axis=0, tiled=True)  23.2 us
    unnamed x42, local copies, waits for them, and re-layouts  19.7 us
    all_to_all x1, starting transfers between devices, local(): lax.all_to_all(slot_send, 'col', split_axis=0, concat_axis=0, tiled=True)  8.54 us
  transfers between devices with their start and end apart: 7, of which 5 were waited for; matrix products, arithmetic and copies ran while one was open for 2% of the time, Pallas kernels for 5%

profile of v2, /device:TPU:12, one launch (start us, length us, event | category | flops | bytes accessed | tf_op | source)
XLA Modules:
  0.0 394.2 jit_solution(13052969807108112651)
XLA Ops:
  10.1 1.6 convert_element_type.14
  12.7 76.7 %handover.1 = (bf16[8,4,64,1536]{3,2,1,0:T(8,128)(2,1)}, bf16[4,64,512]{2,1,0:T(8,128)(2,1)}, bf16[4,1536,512]{2,1,0:T(8,128)(2,1)}) custom-call(bf16[4,64,1536]{2,1,0:T(8,128)(2,1)S(1)} %bitcast.44, bf16[4,64,512]{2,1,0:T(8,128)(2,1)S(1)} %bitcast.48, bf16[1536,512]{1,0:T(8,128)(2,1)S(1)} %copy-done.6), custom_call_target="tpu_custom_call" | custom-call | bytes 300000000 | tf_op jit(solution)/shard_map/handover/pallas_call | solution.py:161
  89.4 30.8 %project.1 = (bf16[1536,512]{1,0:T(8,128)(2,1)S(1)}, bf16[1536,512]{1,0:T(8,128)(2,1)S(1)}, bf16[1536,512]{1,0:T(8,128)(2,1)S(1)}, f32[1536,128]{1,0:T(8,128)S(1)}, bf16[24,2,128,512]{3,2,1,0:T(8,128)(2,1)}) custom-call(s32[3]{0:T(128)S(1)} %copy-done.11, s32[12]{0:T(128)S(1)} %multiply_add_fusion.spots, bf16[4,1536,512]{2,1,0:T(8,128)(2,1)} %get-tuple-element.23.tok, ...), custom_call_target="tpu_custom_call" | custom-call | flops 9663676416 | bytes 30000000 | tf_op jit(solution)/shard_map/project/pallas_call | solution.py:260
  121.4 8.6 %scan.3 = (bf16[512,512]{1,0:T(8,128)(2,1)}, f32[4,128,128]{2,1,0:T(8,128)S(1)}) custom-call(s32[3]{0:T(128)S(1)} %copy-done.11, s32[3,4]{1,0:T(4,128)S(1)} %copy-done.9, bf16[1536,512]{1,0:T(8,128)(2,1)S(1)} %get-tuple-element.28.q_ref, bf16[1536,512]{1,0:T(8,128)(2,1)S(1)} %get-tuple-element.29.k_ref, bf16[1536,512]{1,0:T(8,128)(2,1)} %copy-done.15, ...), custom_call_target="tpu_custom_call" | custom-call | flops 4000000000 | bytes 5000000 | tf_op jit(solution)/shard_map/scan/pallas_call | solution.py:379
  132.7 8.5 %all-to-all-start.3 = ((s32[8,3,1]{1,2,0:T(1,128)}), s32[8,3,1]{1,2,0:T(1,128)S(1)}, u32[]{:S(2)}, u32[]{:S(2)}) async-start(s32[8,3,1]{1,2,0:T(1,128)} %bitcast.63), calls=%async_computation.3 | async-start | bytes 8192 | tf_op jit(solution)/shard_map/all_to_all | solution.py:481
  141.3 1.7 copy.51
  142.9 2.3 all-to-all-done.3
  145.3 6.3 %all-to-all-start.1 = ((bf16[8,64,256]{2,1,0:T(8,128)(2,1)}), bf16[8,64,256]{2,1,0:T(8,128)(2,1)}, u32[]{:S(2)}, u32[]{:S(2)}) async-start(bf16[8,64,256]{2,1,0:T(8,128)(2,1)} %bitcast.62), calls=%async_computation.1 | async-start | bytes 524288 | tf_op jit(solution)/shard_map/all_to_all | solution.py:435
  152.5 5.9 %all-to-all-done.1 = bf16[8,64,256]{2,1,0:T(8,128)(2,1)} async-done(((bf16[8,64,256]{2,1,0:T(8,128)(2,1)}), bf16[8,64,256]{2,1,0:T(8,128)(2,1)}, u32[]{:S(2)}, u32[]{:S(2)}) %all-to-all-start.1) | async-done | bytes 262176 | tf_op jit(solution)/shard_map/all_to_all | solution.py:435
  158.4 23.2 %all_to_all.21 = bf16[8,64,768]{2,1,0:T(8,128)(2,1)} all-to-all(bf16[8,64,768]{2,1,0:T(8,128)(2,1)} %bitcast.59), channel_id=1, replica_groups=mesh['row'=4,'col'=8] {'col'}, dimensions={0} | all-to-all | bytes 1572864 | tf_op jit(solution)/shard_map/all_to_all | solution.py:435
  181.6 6.8 %all-to-all-start.2 = ((bf16[24,2,128,512]{3,2,1,0:T(8,128)(2,1)}), bf16[24,2,128,512]{3,2,1,0:T(8,128)(2,1)}, u32[]{:S(2)}, u32[]{:S(2)}) async-start(bf16[24,2,128,512]{3,2,1,0:T(8,128)(2,1)} %get-tuple-element.39), calls=%async_computation.2 | async-start | bytes 12582912 | tf_op jit(solution)/shard_map/all_to_all | solution.py:490
  190.8 8.5 %scan.4 = (bf16[512,512]{1,0:T(8,128)(2,1)}, f32[4,128,128]{2,1,0:T(8,128)S(1)}) custom-call(s32[3]{0:T(128)S(1)} %copy-done.11, s32[3,4]{1,0:T(4,128)S(1)} %copy-done.9, bf16[1536,512]{1,0:T(8,128)(2,1)S(1)} %get-tuple-element.28.q_ref, bf16[1536,512]{1,0:T(8,128)(2,1)S(1)} %copy-done.13, bf16[1536,512]{1,0:T(8,128)(2,1)} %copy-done.15, ...), custom_call_target="tpu_custom_call" | custom-call | flops 4000000000 | bytes 5000000 | tf_op jit(solution)/shard_map/scan/pallas_call | solution.py:379
  199.4 1.4 copy-done.14
  200.9 8.5 %scan.5 = (bf16[512,512]{1,0:T(8,128)(2,1)}, f32[4,128,128]{2,1,0:T(8,128)S(1)}) custom-call(s32[3]{0:T(128)S(1)} %copy-done.11, s32[3,4]{1,0:T(4,128)S(1)} %copy-done.9, bf16[1536,512]{1,0:T(8,128)(2,1)S(1)} %get-tuple-element.28.q_ref, bf16[1536,512]{1,0:T(8,128)(2,1)S(1)} %copy-done.14, bf16[1536,512]{1,0:T(8,128)(2,1)} %copy-done.15, ...), custom_call_target="tpu_custom_call" | custom-call | flops 4000000000 | bytes 5000000 | tf_op jit(solution)/shard_map/scan/pallas_call | solution.py:379
  212.3 111.4 %all-gather.11.cloned.1.call-done = bf16[32,64,512]{2,1,0:T(8,128)(2,1)} async-done(((bf16[4,64,512]{2,1,0:T(8,128)(2,1)}), bf16[32,64,512]{2,1,0:T(8,128)(2,1)}) %all-gather.11.cloned.1.call-update) | async-done | bytes 2097168 | tf_op jit(solution)/shard_map/all_gather | solution.py:466
  323.7 1.6 copy-done.1
  325.3 1.6 copy-done.3
  328.1 19.9 %all-gather.13.cloned.1.call-done = bf16[2048,512]{1,0:T(8,128)(2,1)} async-done(((bf16[512,512]{1,0:T(8,128)(2,1)}), bf16[2048,512]{1,0:T(8,128)(2,1)}) %all-gather.13.cloned.1.call-update) | async-done | bytes 2097168 | tf_op jit(solution)/shard_map/all_gather | solution.py:496
  348.0 1.6 copy-done.4
  350.8 21.8 %all-gather.15.cloned.1.call-done = bf16[2048,512]{1,0:T(8,128)(2,1)} async-done(((bf16[512,512]{1,0:T(8,128)(2,1)}), bf16[2048,512]{1,0:T(8,128)(2,1)}) %all-gather.15.cloned.1.call-update) | async-done | bytes 2097168 | tf_op jit(solution)/shard_map/all_gather | solution.py:496
  372.6 1.6 copy-done.5
  376.7 3.5 gather_fusion
  380.2 4.9 %copy.39 = bf16[12,128,2,512]{3,2,1,0:T(2,128)(2,1)} copy(bf16[12,128,2,512]{3,1,2,0:T(8,128)(2,1)S(1)} %bitcast.55) | data formatting | bytes 6291456
  386.0 1.7 copy.56
  (69 shorter events, 19.7 us)
Async XLA Ops:
  7.2 4.6 %copy-start.18 = (f32[64,2048]{1,0:T(8,128)S(1)}, f32[64,2048]{1,0:T(8,128)}, u32[]{:S(2)}) copy-start(f32[64,2048]{1,0:T(8,128)} %param.13) | copy-start | bytes 1572868
  7.2 205.1 %all-gather.9.cloned.1.call-start = ((), (), s32[]{:S(2)}) async-start(), calls=%async_computation.4 | async-start | bytes 2621440 | tf_op jit(solution)/shard_map/all_gather | solution.py:496
  10.0 2.6 copy-start.6
  11.7 77.7 %copy-start.7 = (bf16[3,3,1536]{2,1,0:T(4,128)(2,1)S(1)}, bf16[3,3,1536]{2,1,0:T(4,128)(2,1)}, u32[]{:S(2)}) copy-start(bf16[3,3,1536]{2,1,0:T(4,128)(2,1)} %prior.1) | copy-start | bytes 82948
  11.7 77.7 %copy-start.8 = (f32[4,1536]{1,0:T(4,128)S(1)}, f32[4,1536]{1,0:T(4,128)}, u32[]{:S(2)}) copy-start(f32[4,1536]{1,0:T(4,128)} %taps.1) | copy-start | bytes 73732
  11.7 77.7 %copy-start.11 = (s32[3]{0:T(128)S(1)}, s32[3]{0:T(128)}, u32[]{:S(2)}) copy-start(s32[3]{0:T(128)} %lens.7) | copy-start | bytes 40
  89.4 32.0 %copy-start.9 = (s32[3,4]{1,0:T(4,128)S(1)}, s32[3,4]{1,0:T(4,128)}, u32[]{:S(2)}) copy-start(s32[3,4]{1,0:T(4,128)} %picks.5) | copy-start | bytes 148
  89.4 32.0 %copy-start.10 = (f32[512]{0:T(512)S(1)}, f32[512]{0:T(512)}, u32[]{:S(2)}) copy-start(f32[512]{0:T(512)} %param.17) | copy-start | bytes 6148
  120.3 1.1 copy-start.15
  121.4 8.6 %copy-start.12 = (bf16[1536,512]{1,0:T(8,128)(2,1)}, bf16[1536,512]{1,0:T(8,128)(2,1)S(1)}, u32[]{:S(2)}) copy-start(bf16[1536,512]{1,0:T(8,128)(2,1)S(1)} %get-tuple-element.29.k_ref) | copy-start | bytes 4718596
  132.7 12.6 %all-to-all-start.3 = ((s32[8,3,1]{1,2,0:T(1,128)}), s32[8,3,1]{1,2,0:T(1,128)S(1)}, u32[]{:S(2)}, u32[]{:S(2)}) async-start(s32[8,3,1]{1,2,0:T(1,128)} %bitcast.63), calls=%async_computation.3 | async-start | bytes 8192 | tf_op jit(solution)/shard_map/all_to_all | solution.py:481
  145.3 13.1 %all-to-all-start.1 = ((bf16[8,64,256]{2,1,0:T(8,128)(2,1)}), bf16[8,64,256]{2,1,0:T(8,128)(2,1)}, u32[]{:S(2)}, u32[]{:S(2)}) async-start(bf16[8,64,256]{2,1,0:T(8,128)(2,1)} %bitcast.62), calls=%async_computation.1 | async-start | bytes 524288 | tf_op jit(solution)/shard_map/all_to_all | solution.py:435
  181.6 195.1 %all-to-all-start.2 = ((bf16[24,2,128,512]{3,2,1,0:T(8,128)(2,1)}), bf16[24,2,128,512]{3,2,1,0:T(8,128)(2,1)}, u32[]{:S(2)}, u32[]{:S(2)}) async-start(bf16[24,2,128,512]{3,2,1,0:T(8,128)(2,1)} %get-tuple-element.39), calls=%async_computation.2 | async-start | bytes 12582912 | tf_op jit(solution)/shard_map/all_to_all | solution.py:490
  188.4 135.2 %all-gather.11.cloned.1.call-start = ((), (), s32[]{:S(2)}) async-start(), calls=%async_computation.5 | async-start | bytes 2359296 | tf_op jit(solution)/shard_map/all_gather | solution.py:466
  189.2 158.8 %all-gather.13.cloned.1.call-start = ((), (), s32[]{:S(2)}) async-start(), calls=%async_computation.6 | async-start | bytes 2621440 | tf_op jit(solution)/shard_map/all_gather | solution.py:496
  189.4 1.4 copy-start.13
  199.4 173.2 %all-gather.15.cloned.1.call-start = ((), (), s32[]{:S(2)}) async-start(), calls=%async_computation.7 | async-start | bytes 2621440 | tf_op jit(solution)/shard_map/all_gather | solution.py:496
  199.4 1.4 copy-start.14
  323.7 1.6 copy-start.1
  325.3 1.6 copy-start.3
  326.9 21.1 %copy-start.2 = (bf16[32,64,512]{2,1,0:T(8,128)(2,1)S(1)}, bf16[32,64,512]{2,1,0:T(8,128)(2,1)}, u32[]{:S(2)}) copy-start(bf16[32,64,512]{2,1,0:T(8,128)(2,1)} %all-gather.11.cloned.1.call-done) | copy-start | bytes 6291460
  348.0 1.6 copy-start.4
  372.6 1.6 copy-start.5
  380.2 4.9 %copy-start.16 = (bf16[8,64,768]{2,1,0:T(8,128)(2,1)S(1)}, bf16[8,64,768]{2,1,0:T(8,128)(2,1)}, u32[]{:S(2)}) copy-start(bf16[8,64,768]{2,1,0:T(8,128)(2,1)} %all_to_all.21) | copy-start | bytes 2359300
  (2 other events, 1.6 us)
Sparse Core Ops, SparseCore 0:
  130.1 25.4 all-gather.8
  191.4 132.2 all-gather.10
  325.2 22.7 all-gather.12
  350.0 22.5 all-gather.14

commit v3 on v2

--- a/solution.py
+++ b/solution.py
@@ -21,11 +21,11 @@
 
 
 def handover_kernel(
-    chain, in_parts, out_parts, tokens, win, out_rows, tokens_all, own, part_send, part_recv, tok_send, tok_recv,
-    chain_send, chain_recv, pair_send, pair_recv,
+    chain, in_parts, out_parts, in_blocks, out_blocks, tokens, win, out_rows, server_in, server_out, tokens_all, own, part_send, part_recv, tok_send, tok_recv,
+    chain_send, chain_recv, pair_send, pair_recv, block_send, block_recv,
 ):
     row, col = lax.axis_index("row"), lax.axis_index("col")
-    rows = in_parts.shape[0]
+    rows, cols = in_parts.shape[0], in_blocks.shape[0]
     place, side = col // 2, col % 2
     twin = row + 1 - 2 * (row % 2)
     across = lax.rem(row + 2, rows)
@@ -36,18 +36,9 @@
     barrier = pltpu.get_barrier_semaphore()
     for d in range(1, rows):
         pl.semaphore_signal(barrier, inc=1, device_id=(lax.rem(row + d, rows), col), device_id_type=MESH)
-    pl.semaphore_signal(barrier, inc=1, device_id=(row, partner), device_id_type=MESH)
-
-    @pl.when(place > 0)
-    def _():
-        pl.semaphore_signal(barrier, inc=1, device_id=(row, col - 2), device_id_type=MESH)
-
-    @pl.when(place < chain - 1)
-    def _():
-        pl.semaphore_signal(barrier, inc=1, device_id=(row, col + 2), device_id_type=MESH)
-
-    neighbours = lax.div(place + chain - 1, chain) + lax.div(2 * (chain - 1) - place, chain)
-    pl.semaphore_wait(barrier, rows + neighbours)
+    for d in range(1, cols):
+        pl.semaphore_signal(barrier, inc=1, device_id=(row, lax.rem(col + d, cols)), device_id_type=MESH)
+    pl.semaphore_wait(barrier, rows - 1 + cols - 1)
 
     def remote(src, dst, send, recv, target):
         return pltpu.make_async_remote_copy(
@@ -69,6 +60,8 @@
         pltpu.make_async_copy(in_parts.at[row], win.at[col, row], own.at[0]),
         pltpu.make_async_copy(out_parts.at[row], out_rows.at[row], own.at[1]),
         pltpu.make_async_copy(tokens, tokens_all.at[row], own.at[2]),
+        pltpu.make_async_copy(in_blocks.at[col], server_in.at[col], own.at[3]),
+        pltpu.make_async_copy(out_blocks.at[col], server_out.at[col], own.at[4]),
     ]
     for copy in own_copies:
         copy.start()
@@ -126,6 +119,17 @@
         if 0 < s <= chunks:
             token_copy(0, s - 1).wait_recv()
             token_copy(2, s - 1).start()
+    block_copies = []
+    for d in range(1, cols):
+        peer = lax.rem(col + d, cols)
+        block_copies.append(
+            remote(in_blocks.at[peer], server_in.at[col], block_send.at[0, d], block_recv.at[0, d], (row, peer))
+        )
+        block_copies.append(
+            remote(out_blocks.at[peer], server_out.at[col], block_send.at[1, d], block_recv.at[1, d], (row, peer))
+        )
+    for copy in block_copies:
+        copy.start()
     for n in range(max(0, chain - 1), chunks):
         token_copy(0, n).wait_recv()
         token_copy(2, n).start()
@@ -137,8 +141,8 @@
     for d in range(1, rows):
         part_copies[2 * (d - 1)].wait_send()
         part_copies[2 * (d - 1) + 1].wait()
-    own_copies[1].wait()
-    own_copies[2].wait()
+    for copy in own_copies[1:]:
+        copy.wait()
     for s in range(chain):
         for way in range(2):
 
@@ -151,8 +155,11 @@
                 if s > 0 or way == 0:
                     pair_copy(way, s).wait()
 
-
-def handover(in_parts, out_parts, tokens, cols):
+    for copy in block_copies:
+        copy.wait()
+
+
+def handover(in_parts, out_parts, in_blocks, out_blocks, tokens, cols):
     rows, depth, width = in_parts.shape
     chain = cols // 2
     chunks = tokens.shape[0] // SEQ
@@ -160,15 +167,17 @@
     anywhere = pl.BlockSpec(memory_space=pl.ANY)
     return pl.pallas_call(
         functools.partial(handover_kernel, chain),
-        in_specs=[anywhere] * 3,
-        out_specs=[anywhere] * 3,
+        in_specs=[anywhere] * 5,
+        out_specs=[anywhere] * 5,
         out_shape=[
             jax.ShapeDtypeStruct((cols, rows, depth, width), BF),
             jax.ShapeDtypeStruct(out_parts.shape, BF),
+            jax.ShapeDtypeStruct(in_blocks.shape, BF),
+            jax.ShapeDtypeStruct(out_blocks.shape, BF),
             jax.ShapeDtypeStruct((rows,) + tokens.shape, BF),
         ],
         scratch_shapes=[
-            dma((3,)),
+            dma((5,)),
             dma((2, rows)),
             dma((2, rows)),
             dma((3, chunks)),
@@ -177,13 +186,72 @@
             dma((2, chain)),
             dma((2, chain)),
             dma((2, chain)),
+            dma((2, cols)),
+            dma((2, cols)),
         ],
         compiler_params=pltpu.CompilerParams(
             collective_id=0, has_side_effects=True, vmem_limit_bytes=VMEM_LIMIT
         ),
         cost_estimate=pl.CostEstimate(flops=0, bytes_accessed=300_000_000, transcendentals=0),
         name="handover",
-    )(in_parts, out_parts, tokens)
+    )(in_parts, out_parts, in_blocks, out_blocks, tokens)
+
+
+def row_gather_kernel(mine, whole, own, send, recv):
+    row, col = lax.axis_index("row"), lax.axis_index("col")
+    rows = whole.shape[0]
+    twin = row + 1 - 2 * (row % 2)
+    across = lax.rem(row + 2, rows)
+    chunks = send.shape[1]
+    span = mine.shape[0] // chunks
+
+    barrier = pltpu.get_barrier_semaphore()
+    for peer in (twin, across):
+        pl.semaphore_signal(barrier, inc=1, device_id=(peer, col), device_id_type=MESH)
+    pl.semaphore_wait(barrier, 2)
+
+    def copy(kind, n):
+        piece = pl.ds(n * span, span)
+        slot = across if kind == 2 else row
+        return pltpu.make_async_remote_copy(
+            src_ref=whole.at[across, piece] if kind == 2 else mine.at[piece],
+            dst_ref=whole.at[slot, piece],
+            send_sem=send.at[kind, n],
+            recv_sem=recv.at[kind, n],
+            device_id=(across if kind == 0 else twin, col),
+            device_id_type=MESH,
+        )
+
+    local_copy = pltpu.make_async_copy(mine, whole.at[row], own)
+    for kind in range(2):
+        for n in range(chunks):
+            copy(kind, n).start()
+    local_copy.start()
+    for n in range(chunks):
+        copy(0, n).wait_recv()
+        copy(2, n).start()
+    for n in range(chunks):
+        copy(0, n).wait_send()
+        copy(1, n).wait()
+        copy(2, n).wait()
+    local_copy.wait()
+
+
+def row_gather(mine, rows):
+    chunks = mine.shape[0] // SEQ
+    dma = pltpu.SemaphoreType.DMA
+    return pl.pallas_call(
+        row_gather_kernel,
+        in_specs=[pl.BlockSpec(memory_space=pl.ANY)],
+        out_specs=pl.BlockSpec(memory_space=pl.ANY),
+        out_shape=jax.ShapeDtypeStruct((rows,) + mine.shape, BF),
+        scratch_shapes=[dma(()), dma((3, chunks)), dma((3, chunks))],
+        compiler_params=pltpu.CompilerParams(
+            collective_id=1, has_side_effects=True, vmem_limit_bytes=VMEM_LIMIT
+        ),
+        cost_estimate=pl.CostEstimate(flops=0, bytes_accessed=100_000_000, transcendentals=0),
+        name="row_gather",
+    )(mine)
 
 
 def project_kernel(
@@ -313,7 +381,8 @@
     return lax.dot_general(a, b, (((0,), (0,)), ((), ())), preferred_element_type=F32)
 
 
-def scan_kernel(prompt, lens, picks, q_ref, k_ref, v_ref, rates, pool, gain, normed, state_out):
+def scan_kernel(lens, picks, q_ref, k_ref, v_ref, rates, pool, gain, normed, state_out):
+    prompt = pl.program_id(0)
     heads = pool.shape[1]
     size = PAGE
     blocks = SEQ // size
@@ -370,37 +439,38 @@
                 out * scale * gain[:, h * DK : (h + 1) * DK]
             ).astype(BF)
     for h in range(heads):
-        state_out[h] = states[h]
-
-
-def scan_prompt(prompt, lengths, picks, query, key, value, rates, pool, gain):
+        state_out[0, h] = states[h]
+
+
+def scan_all(lengths, picks, query, key, value, rates, pool, gain):
     heads = pool.shape[1]
-    wide = pl.BlockSpec((SEQ, heads * DK), lambda i, *_: (prompt, 0))
+    prompts = query.shape[0] // SEQ
+    wide = pl.BlockSpec((SEQ, heads * DK), lambda i, *_: (i, 0))
     return pl.pallas_call(
-        functools.partial(scan_kernel, prompt),
+        scan_kernel,
         grid_spec=pltpu.PrefetchScalarGridSpec(
             num_scalar_prefetch=2,
-            grid=(1,),
+            grid=(prompts,),
             in_specs=[
                 wide,
                 wide,
                 wide,
-                pl.BlockSpec((SEQ, DK), lambda i, *_: (prompt, 0)),
+                pl.BlockSpec((SEQ, DK), lambda i, *_: (i, 0)),
                 pl.BlockSpec(pool.shape, lambda i, *_: (0, 0, 0, 0)),
                 pl.BlockSpec((1, heads * DK), lambda i, *_: (0, 0)),
             ],
             out_specs=[
-                pl.BlockSpec((SEQ, heads * DK), lambda i, *_: (0, 0)),
-                pl.BlockSpec((heads, DK, DK), lambda i, *_: (0, 0, 0)),
+                wide,
+                pl.BlockSpec((1, heads, DK, DK), lambda i, *_: (i, 0, 0, 0)),
             ],
         ),
         out_shape=[
-            jax.ShapeDtypeStruct((SEQ, heads * DK), BF),
-            jax.ShapeDtypeStruct((heads, DK, DK), F32),
+            jax.ShapeDtypeStruct(query.shape, BF),
+            jax.ShapeDtypeStruct((prompts, heads, DK, DK), F32),
         ],
         compiler_params=pltpu.CompilerParams(vmem_limit_bytes=VMEM_LIMIT),
         cost_estimate=pl.CostEstimate(
-            flops=4_000_000_000, bytes_accessed=5_000_000, transcendentals=2048
+            flops=12_000_000_000, bytes_accessed=5_000_000, transcendentals=2048
         ),
         name="scan",
     )(lengths, picks, query, key, value, rates, pool, gain)
@@ -419,6 +489,12 @@
     width = wout.shape[3]
     return pl.pallas_call(
         out_kernel,
+        grid=(tokens // SEQ,),
+        in_specs=[
+            pl.BlockSpec((rows, SEQ, span), lambda i: (0, i, 0)),
+            pl.BlockSpec(wout.shape, lambda i: (0, 0, 0, 0)),
+        ],
+        out_specs=pl.BlockSpec((SEQ, width), lambda i: (i, 0)),
         out_shape=jax.ShapeDtypeStruct((tokens, width), BF),
         compiler_params=pltpu.CompilerParams(vmem_limit_bytes=VMEM_LIMIT),
         cost_estimate=pl.CostEstimate(
@@ -428,13 +504,9 @@
     )(heads_all, wout)
 
 
-def col_exchange(weight):
+def col_blocks(weight, cols):
     rows, width = weight.shape
-    cols = lax.axis_size("col")
-    parts = weight.reshape(rows, cols, width // cols).transpose(1, 0, 2)
-    return lax.all_to_all(parts, "col", split_axis=0, concat_axis=0, tiled=True).reshape(
-        rows * cols, width // cols
-    )
+    return weight.reshape(rows, cols, width // cols).transpose(1, 0, 2)
 
 
 def local(
@@ -462,7 +534,11 @@
     trainer_out = out_weight.astype(BF)
     in_parts = trainer_in.reshape(depth, row_count, -1).transpose(1, 0, 2)
     out_parts = trainer_out.reshape(depth, row_count, -1).transpose(1, 0, 2)
-    win, out_rows, tokens_all = handover(in_parts, out_parts, tokens, col_count)
+    win, out_rows, server_in, server_out, tokens_all = handover(
+        in_parts, out_parts, col_blocks(trainer_in, col_count), col_blocks(trainer_out, col_count), tokens, col_count
+    )
+    server_in = server_in.reshape(-1, server_in.shape[2])
+    server_out = server_out.reshape(-1, server_out.shape[2])
     wout = lax.all_gather(out_rows, "col", axis=0)
 
     my_beta = lax.dynamic_slice_in_dim(beta_weight, row_id * heads, heads, 1).astype(BF)
@@ -471,32 +547,27 @@
     pages_dev = prompts * PAGES_SEQ
     capacity = max(1, 2 * pages_dev // col_count)
     slots = capacity * col_count
-    targets = page_table[:, :, 0].reshape(-1)
-    slot_ids = page_table[:, :, 1].reshape(-1)
+    table = lax.all_gather(page_table.reshape(pages_dev, 2), "col", axis=0)
+    targets, slot_ids = table[:, :, 0], table[:, :, 1]
     order = jnp.arange(pages_dev, dtype=jnp.int32)
-    earlier = (targets[:, None] == targets[None, :]) & (order[None, :] < order[:, None])
-    spots = targets * capacity + jnp.sum(earlier.astype(jnp.int32), axis=1)
-    held = spots[None, :] == jnp.arange(slots, dtype=jnp.int32)[:, None]
-    slot_send = jnp.sum(jnp.where(held, slot_ids[None, :] - pages_dev, 0), axis=1) + pages_dev
-    arrived_slots = lax.all_to_all(slot_send, "col", split_axis=0, concat_axis=0, tiled=True)
-    sources = jnp.argmax(arrived_slots[None, :] == order[:, None], axis=1).astype(jnp.int32)
+    earlier = (targets[:, :, None] == targets[:, None, :]) & (order[None, :] < order[:, None])
+    ranks = jnp.sum(earlier.astype(jnp.int32), axis=2)
+    col_id = lax.axis_index("col")
+    my_targets = page_table[:, :, 0].reshape(-1)
+    my_earlier = (my_targets[:, None] == my_targets[None, :]) & (order[None, :] < order[:, None])
+    spots = my_targets * capacity + jnp.sum(my_earlier.astype(jnp.int32), axis=1)
+    places = jnp.arange(col_count, dtype=jnp.int32)[:, None] * capacity + ranks
+    mine = (targets == col_id)[None] & (slot_ids[None] == order[:, None, None])
+    sources = jnp.sum(jnp.where(mine, places[None], 0), axis=(1, 2))
 
     query, key, value, rates, outgoing = project(
         tokens_all, win, wbeta, conv_weight, conv_prior, lengths, spots, slots
     )
-    trainer_in, trainer_out, rates = lax.optimization_barrier((trainer_in, trainer_out, rates))
-    server_in = col_exchange(trainer_in)
-    server_out = col_exchange(trainer_out)
     arrived = lax.all_to_all(outgoing, "col", split_axis=0, concat_axis=0, tiled=True)
 
     gain = head_gain.reshape(1, -1)
-    layer_parts, state_parts = [], []
-    for p in range(prompts):
-        normed, state = scan_prompt(p, lengths, state_index, query, key, value, rates, state_pool, gain)
-        layer_parts.append(out_project(lax.all_gather(normed, "row", axis=0), wout))
-        state_parts.append(state)
-    layer_out = jnp.concatenate(layer_parts, axis=0)
-    final_state = jnp.stack(state_parts, axis=0)
+    normed, final_state = scan_all(lengths, state_index, query, key, value, rates, state_pool, gain)
+    layer_out = out_project(row_gather(normed, row_count), wout)
     page_cache = jnp.take(arrived, sources, axis=0, mode="clip").transpose(0, 2, 1, 3)
     return (server_in, server_out, layer_out, final_state, page_cache)
 

time: 397 us -> 345 us (0.87)
  waiting for transfers between devices: 162 us -> 0.73 us
  blocking collectives: 23.2 us -> 109 us
  Pallas kernels: 137 us -> 188 us
  starting transfers between devices: 22 us -> 8.69 us
  local copies, waits for them, and re-layouts: 28.7 us -> 21.6 us
  other arithmetic: 7.42 us -> 2.52 us
    all_gather x1, waiting for transfers between devices: 111 us -> 0.02 us  [local(): wout = lax.all_gather(out_rows, 'col', axis=0)]
    all_gather x0 -> x1, blocking collectives: none -> 109 us  [local(): table = lax.all_gather(page_table.reshape(pages_dev, 2), 'col', axis=0)]
    all_gather x3 -> x0, waiting for transfers between devices: 41.7 us -> none  [local(): layer_parts.append(out_project(lax.all_gather(normed, 'row', axis=0), wout))]
    pallas_call x6 -> x3, Pallas kernels: 29.4 us -> 66.6 us  [the longest x1 40.3 us: row_gather(): pl.pallas_call(row_gather_kernel, in_specs=[pl.BlockSpec(memory_space=pl....]
    all_to_all x1 -> x0, blocking collectives: 23.2 us -> none  [col_exchange(): lax.all_to_all(parts, 'col', split_axis=0, concat_axis=0, tiled=True)]
    all_to_all x2 -> x0, starting transfers between devices: 14.8 us -> none  [the longest x1 8.54 us: local(): lax.all_to_all(slot_send, 'col', split_axis=0, concat_axis=0, tiled=True)]
    pallas_call x1, Pallas kernels: 76.7 us -> 90 us  [handover(): pl.pallas_call(functools.partial(handover_kernel, chain), in_specs=[anywh...]
    all_to_all x2 -> x0, waiting for transfers between devices: 8.2 us -> none  [the longest x1 5.85 us: col_exchange(): lax.all_to_all(parts, 'col', split_axis=0, concat_axis=0, tiled=True)]
  transfers between devices with their start and end apart: 7 -> 2, of which waited for: 5 -> 0; matrix products, arithmetic and copies ran while one was open for 2% -> 0% of each run, Pallas kernels for 5% -> 19%
where the time goes in v3:
time: 345 us
  Pallas kernels  188 us (54%)
  blocking collectives  109 us (32%)
  local copies, waits for them, and re-layouts  21.6 us (6%)
  between operations  14.3 us (4%)
  starting transfers between devices  8.69 us (3%)
    all_gather x1, blocking collectives, local(): table = lax.all_gather(page_table.reshape(pages_dev, 2), 'col', axis=0)  109 us
    pallas_call x1, Pallas kernels, handover(): pl.pallas_call(functools.partial(handover_kernel, chain), in_specs=[anywh...  90 us
    pallas_call x1, Pallas kernels, row_gather(): pl.pallas_call(row_gather_kernel, in_specs=[pl.BlockSpec(memory_space=pl....  40.3 us
    pallas_call x1, Pallas kernels, project(): pl.pallas_call(project_kernel, grid_spec=pltpu.PrefetchScalarGridSpec(num...  30.9 us
    pallas_call x1, Pallas kernels, scan_all(): pl.pallas_call(scan_kernel, grid_spec=pltpu.PrefetchScalarGridSpec(num_sc...  19.6 us
    unnamed x41, local copies, waits for them, and re-layouts  15.7 us
    all_to_all x1, starting transfers between devices, local(): lax.all_to_all(outgoing, 'col', split_axis=0, concat_axis=0, tiled=True)  8.69 us
  transfers between devices with their start and end apart: 2, of which 0 were waited for; matrix products, arithmetic and copies ran while one was open for 0% of the time, Pallas kernels for 19%

profile of v3, /device:TPU:12, one launch (start us, length us, event | category | flops | bytes accessed | tf_op | source)
XLA Modules:
  0.0 344.7 jit_solution(16516865272751744774)
XLA Ops:
  7.2 0.9 copy-done
  8.1 1.1 copy.57
  9.2 1.5 convert_element_type.17
  10.9 0.7 copy.71
  11.9 1.1 pad.4.wbeta
  13.1 0.9 copy-done.2
  14.1 90.0 %handover.1 = (bf16[8,4,64,1536]{3,2,1,0:T(8,128)(2,1)}, bf16[4,64,512]{2,1,0:T(8,128)(2,1)}, bf16[8,64,768]{2,1,0:T(8,128)(2,1)S(1)}, bf16[8,64,256]{2,1,0:T(8,128)(2,1)S(1)}, bf16[4,1536,512]{2,1,0:T(8,128)(2,1)}) custom-call(bf16[4,64,1536]{2,1,0:T(8,128)(2,1)S(1)} %bitcast.42, bf16[4,64,512]{2,1,0:T(8,128)(2,1)S(1)} %bitcast.44, ...), custom_call_target="tpu_custom_call" | custom-call | bytes 300000000 | tf_op jit(solution)/shard_map/handover/pallas_call | solution.py:168
  104.1 0.9 copy-done.3
  105.0 0.7 copy-done.5
  105.7 30.9 %project.1 = (bf16[1536,512]{1,0:T(8,128)(2,1)S(1)}, bf16[1536,512]{1,0:T(8,128)(2,1)S(1)}, bf16[1536,512]{1,0:T(8,128)(2,1)S(1)}, f32[1536,128]{1,0:T(8,128)S(1)}, bf16[24,2,128,512]{3,2,1,0:T(8,128)(2,1)}) custom-call(s32[3]{0:T(128)S(1)} %copy-done.12, s32[12]{0:T(128)S(1)} %multiply_add_fusion.spots, bf16[4,1536,512]{2,1,0:T(8,128)(2,1)} %get-tuple-element.19.tok, ...), custom_call_target="tpu_custom_call" | custom-call | flops 9663676416 | bytes 30000000 | tf_op jit(solution)/shard_map/project/pallas_call | solution.py:328
  136.6 1.1 copy-done.13
  137.7 0.9 copy-done.14
  138.6 8.7 %all-to-all-start = ((bf16[24,2,128,512]{3,2,1,0:T(8,128)(2,1)}), bf16[24,2,128,512]{3,2,1,0:T(8,128)(2,1)}, u32[]{:S(2)}, u32[]{:S(2)}) async-start(bf16[24,2,128,512]{3,2,1,0:T(8,128)(2,1)} %get-tuple-element.28), calls=%async_computation | async-start | bytes 12582912 | tf_op jit(solution)/shard_map/all_to_all | solution.py:566
  147.3 0.7 all-gather.3.cloned.1.call-update
  148.0 1.1 copy-done.15
  149.1 19.6 %scan.1 = (bf16[1536,512]{1,0:T(8,128)(2,1)S(1)}, f32[3,4,128,128]{3,2,1,0:T(8,128)}) custom-call(s32[3]{0:T(128)S(1)} %copy-done.12, s32[3,4]{1,0:T(4,128)S(1)} %copy-done.10, bf16[1536,512]{1,0:T(8,128)(2,1)S(1)} %get-tuple-element.21.q_ref, bf16[1536,512]{1,0:T(8,128)(2,1)S(1)} %get-tuple-element.22.k_ref, bf16[1536,512]{1,0:T(8,128)(2,1)} %copy-done.13, ...), custom_call_target="tpu_custom_call" | custom-call | flops 12000000000 | bytes 5000000 | tf_op jit(solution)/shard_map/scan/pallas_call | solution.py:449
  168.8 40.3 %row_gather.1.heads_all = bf16[4,1536,512]{2,1,0:T(8,128)(2,1)} custom-call(bf16[1536,512]{1,0:T(8,128)(2,1)S(1)} %get-tuple-element.25.mine), custom_call_target="tpu_custom_call" | custom-call | bytes 100000000 | tf_op jit(solution)/shard_map/row_gather/pallas_call | solution.py:243
  209.2 109.4 %all_gather.11 = s32[8,12,2]{1,2,0:T(2,128)S(1)} all-gather(s32[1,12,2]{1,2,0:T(2,128)S(1)} %all_gather_reshape.3), channel_id=1, replica_groups=mesh['row'=4,'col'=8] {'col'}, dimensions={0}, use_global_device_ids=true | all-gather | bytes 864 | tf_op jit(solution)/shard_map/all_gather | solution.py:550
  319.6 1.6 copy-done.7
  321.2 6.7 %out_project.1 = bf16[1536,512]{1,0:T(8,128)(2,1)} custom-call(bf16[4,1536,512]{2,1,0:T(8,128)(2,1)} %row_gather.1.heads_all, bf16[8,4,64,512]{3,2,1,0:T(8,128)(2,1)S(1)} %bitcast.47), custom_call_target="tpu_custom_call" | custom-call | flops 3221225472 | bytes 5000000 | tf_op jit(solution)/shard_map/out_project/pallas_call | solution.py:490
  327.8 3.5 %gather_fusion = bf16[12,2,128,512]{3,2,1,0:T(8,128)(2,1)S(1)} fusion(bf16[24,2,128,512]{3,2,1,0:T(8,128)(2,1)} %all-to-all-done, s32[1024]{0:T(1024)S(1)} %pad_clamp_fusion), kind=kCustom, calls=%fused_computation | custom fusion | bytes 6291504 | tf_op jit(solution)/shard_map/jit(_take)/gather | solution.py:571
  331.4 4.9 %copy.56 = bf16[12,128,2,512]{3,2,1,0:T(2,128)(2,1)} copy(bf16[12,128,2,512]{3,1,2,0:T(8,128)(2,1)S(1)} %bitcast.49) | data formatting | bytes 6291456
  336.3 0.9 copy.74
  337.2 0.7 copy.75
  (52 shorter events, 1.6 us)
Async XLA Ops:
  7.2 0.9 copy-start
  9.1 1.7 copy-start.16
  9.1 2.5 copy-start.17
  10.7 2.4 copy-start.1
  10.8 94.8 %copy-start.12 = (s32[3]{0:T(128)S(1)}, s32[3]{0:T(128)}, u32[]{:S(2)}) copy-start(s32[3]{0:T(128)} %lens.3) | copy-start | bytes 40
  11.8 93.9 %copy-start.8 = (bf16[3,3,1536]{2,1,0:T(4,128)(2,1)S(1)}, bf16[3,3,1536]{2,1,0:T(4,128)(2,1)}, u32[]{:S(2)}) copy-start(bf16[3,3,1536]{2,1,0:T(4,128)(2,1)} %prior.1) | copy-start | bytes 82948
  11.8 93.9 %copy-start.9 = (f32[4,1536]{1,0:T(4,128)S(1)}, f32[4,1536]{1,0:T(4,128)}, u32[]{:S(2)}) copy-start(f32[4,1536]{1,0:T(4,128)} %taps.1) | copy-start | bytes 73732
  13.1 1.0 copy-start.2
  104.1 0.9 copy-start.3
  105.0 0.7 copy-start.5
  136.5 1.1 copy-start.13
  137.7 0.9 copy-start.14
  138.6 9.4 %copy-start.10 = (s32[3,4]{1,0:T(4,128)S(1)}, s32[3,4]{1,0:T(4,128)}, u32[]{:S(2)}) copy-start(s32[3,4]{1,0:T(4,128)} %picks.1) | copy-start | bytes 148
  138.6 9.4 %copy-start.11 = (f32[512]{0:T(512)S(1)}, f32[512]{0:T(512)}, u32[]{:S(2)}) copy-start(f32[512]{0:T(512)} %param.17) | copy-start | bytes 6148
  138.6 189.3 %all-to-all-start = ((bf16[24,2,128,512]{3,2,1,0:T(8,128)(2,1)}), bf16[24,2,128,512]{3,2,1,0:T(8,128)(2,1)}, u32[]{:S(2)}, u32[]{:S(2)}) async-start(bf16[24,2,128,512]{3,2,1,0:T(8,128)(2,1)} %get-tuple-element.28), calls=%async_computation | async-start | bytes 12582912 | tf_op jit(solution)/shard_map/all_to_all | solution.py:566
  147.3 172.3 %all-gather.3.cloned.1.call-start = ((), (), s32[]{:S(2)}) async-start(), calls=%async_computation.1 | async-start | bytes 2359296 | tf_op jit(solution)/shard_map/all_gather | solution.py:542
  148.0 1.1 copy-start.15
  319.6 1.6 copy-start.7
  331.4 4.9 %copy-start.4 = (bf16[8,64,768]{2,1,0:T(8,128)(2,1)S(1)}, bf16[8,64,768]{2,1,0:T(8,128)(2,1)}, u32[]{:S(2)}) copy-start(bf16[8,64,768]{2,1,0:T(8,128)(2,1)} %copy-done.3) | copy-start | bytes 2359300
  331.4 5.8 %copy-start.6 = (bf16[8,64,256]{2,1,0:T(8,128)(2,1)S(1)}, bf16[8,64,256]{2,1,0:T(8,128)(2,1)}, u32[]{:S(2)}) copy-start(bf16[8,64,256]{2,1,0:T(8,128)(2,1)} %copy-done.5) | copy-start | bytes 786436
Sparse Core Ops, SparseCore 0:
  150.2 134.7 all-gather.2

commit v4 on v3

--- a/solution.py
+++ b/solution.py
@@ -21,7 +21,7 @@
 
 
 def handover_kernel(
-    chain, in_parts, out_parts, in_blocks, out_blocks, tokens, win, out_rows, server_in, server_out, tokens_all, own, part_send, part_recv, tok_send, tok_recv,
+    chain, in_parts, in_blocks, out_blocks, tokens, win, server_in, server_out, tokens_all, own, part_send, part_recv, tok_send, tok_recv,
     chain_send, chain_recv, pair_send, pair_recv, block_send, block_recv,
 ):
     row, col = lax.axis_index("row"), lax.axis_index("col")
@@ -51,17 +51,13 @@
         part_copies.append(
             remote(in_parts.at[peer], win.at[col, row], part_send.at[0, d], part_recv.at[0, d], (peer, col))
         )
-        part_copies.append(
-            remote(out_parts.at[peer], out_rows.at[row], part_send.at[1, d], part_recv.at[1, d], (peer, col))
-        )
     for copy in part_copies:
         copy.start()
     own_copies = [
         pltpu.make_async_copy(in_parts.at[row], win.at[col, row], own.at[0]),
-        pltpu.make_async_copy(out_parts.at[row], out_rows.at[row], own.at[1]),
-        pltpu.make_async_copy(tokens, tokens_all.at[row], own.at[2]),
-        pltpu.make_async_copy(in_blocks.at[col], server_in.at[col], own.at[3]),
-        pltpu.make_async_copy(out_blocks.at[col], server_out.at[col], own.at[4]),
+        pltpu.make_async_copy(tokens, tokens_all.at[row], own.at[1]),
+        pltpu.make_async_copy(in_blocks.at[col], server_in.at[col], own.at[2]),
+        pltpu.make_async_copy(out_blocks.at[col], server_out.at[col], own.at[3]),
     ]
     for copy in own_copies:
         copy.start()
@@ -100,7 +96,7 @@
 
     own_copies[0].wait()
     for d in range(1, rows):
-        part_copies[2 * (d - 1)].wait_recv()
+        part_copies[d - 1].wait_recv()
     for s in range(chain):
         for way in range(2):
 
@@ -139,8 +135,7 @@
         for kind in range(3):
             token_copy(kind, n).wait_send()
     for d in range(1, rows):
-        part_copies[2 * (d - 1)].wait_send()
-        part_copies[2 * (d - 1) + 1].wait()
+        part_copies[d - 1].wait_send()
     for copy in own_copies[1:]:
         copy.wait()
     for s in range(chain):
@@ -159,7 +154,7 @@
         copy.wait()
 
 
-def handover(in_parts, out_parts, in_blocks, out_blocks, tokens, cols):
+def handover(in_parts, in_blocks, out_blocks, tokens, cols):
     rows, depth, width = in_parts.shape
     chain = cols // 2
     chunks = tokens.shape[0] // SEQ
@@ -167,17 +162,16 @@
     anywhere = pl.BlockSpec(memory_space=pl.ANY)
     return pl.pallas_call(
         functools.partial(handover_kernel, chain),
-        in_specs=[anywhere] * 5,
-        out_specs=[anywhere] * 5,
+        in_specs=[anywhere] * 4,
+        out_specs=[anywhere] * 4,
         out_shape=[
             jax.ShapeDtypeStruct((cols, rows, depth, width), BF),
-            jax.ShapeDtypeStruct(out_parts.shape, BF),
             jax.ShapeDtypeStruct(in_blocks.shape, BF),
             jax.ShapeDtypeStruct(out_blocks.shape, BF),
             jax.ShapeDtypeStruct((rows,) + tokens.shape, BF),
         ],
         scratch_shapes=[
-            dma((5,)),
+            dma((4,)),
             dma((2, rows)),
             dma((2, rows)),
             dma((3, chunks)),
@@ -194,7 +188,7 @@
         ),
         cost_estimate=pl.CostEstimate(flops=0, bytes_accessed=300_000_000, transcendentals=0),
         name="handover",
-    )(in_parts, out_parts, in_blocks, out_blocks, tokens)
+    )(in_parts, in_blocks, out_blocks, tokens)
 
 
 def row_gather_kernel(mine, whole, own, send, recv):
@@ -320,7 +314,8 @@
 
 def project(tokens_all, win, wbeta, taps, prior, lengths, spots, slots):
     rows, local_tokens, span = tokens_all.shape
-    cols, _, depth, width = win.shape
+    cols, _, depth, _ = win.shape
+    width = taps.shape[1]
     heads = width // (3 * DK)
     prompts = local_tokens // SEQ
     flat = jax.ShapeDtypeStruct((local_tokens, heads * DK), BF)
@@ -484,15 +479,15 @@
     out[...] = total.astype(BF)
 
 
-def out_project(heads_all, wout):
+def out_project(heads_all, wout, skip):
     rows, tokens, span = heads_all.shape
-    width = wout.shape[3]
+    width = wout.shape[3] - skip
     return pl.pallas_call(
         out_kernel,
         grid=(tokens // SEQ,),
         in_specs=[
             pl.BlockSpec((rows, SEQ, span), lambda i: (0, i, 0)),
-            pl.BlockSpec(wout.shape, lambda i: (0, 0, 0, 0)),
+            pl.BlockSpec(wout.shape[:3] + (width,), lambda i: (0, 0, 0, skip // width)),
         ],
         out_specs=pl.BlockSpec((SEQ, width), lambda i: (i, 0)),
         out_shape=jax.ShapeDtypeStruct((tokens, width), BF),
@@ -534,12 +529,15 @@
     trainer_out = out_weight.astype(BF)
     in_parts = trainer_in.reshape(depth, row_count, -1).transpose(1, 0, 2)
     out_parts = trainer_out.reshape(depth, row_count, -1).transpose(1, 0, 2)
-    win, out_rows, server_in, server_out, tokens_all = handover(
-        in_parts, out_parts, col_blocks(trainer_in, col_count), col_blocks(trainer_out, col_count), tokens, col_count
+    win, server_in, server_out, tokens_all = handover(
+        jnp.concatenate([in_parts, out_parts], axis=2),
+        col_blocks(trainer_in, col_count),
+        col_blocks(trainer_out, col_count),
+        tokens,
+        col_count,
     )
     server_in = server_in.reshape(-1, server_in.shape[2])
     server_out = server_out.reshape(-1, server_out.shape[2])
-    wout = lax.all_gather(out_rows, "col", axis=0)
 
     my_beta = lax.dynamic_slice_in_dim(beta_weight, row_id * heads, heads, 1).astype(BF)
     wbeta = jnp.pad(my_beta, ((0, 0), (0, DK - heads)))
@@ -548,6 +546,7 @@
     capacity = max(1, 2 * pages_dev // col_count)
     slots = capacity * col_count
     table = lax.all_gather(page_table.reshape(pages_dev, 2), "col", axis=0)
+    table, tokens_all = lax.optimization_barrier((table, tokens_all))
     targets, slot_ids = table[:, :, 0], table[:, :, 1]
     order = jnp.arange(pages_dev, dtype=jnp.int32)
     earlier = (targets[:, :, None] == targets[:, None, :]) & (order[None, :] < order[:, None])
@@ -567,7 +566,7 @@
 
     gain = head_gain.reshape(1, -1)
     normed, final_state = scan_all(lengths, state_index, query, key, value, rates, state_pool, gain)
-    layer_out = out_project(row_gather(normed, row_count), wout)
+    layer_out = out_project(row_gather(normed, row_count), win, conv_weight.shape[1])
     page_cache = jnp.take(arrived, sources, axis=0, mode="clip").transpose(0, 2, 1, 3)
     return (server_in, server_out, layer_out, final_state, page_cache)
 

time: 345 us -> 337 us (0.977); the launches traced: 345 us -> 332 us
  blocking collectives: 109 us -> 14.3 us
  waiting for transfers between devices: 0.73 us -> 66.3 us
  Pallas kernels: 188 us -> 215 us
  between operations: 14.3 us -> 0.86 us
    all_gather x1, blocking collectives: 109 us -> 14.3 us  [local(): table = lax.all_gather(page_table.reshape(pages_dev, 2), 'col', axis=0)]
    all_to_all x1, waiting for transfers between devices: 0.01 us -> 66.3 us  [local(): lax.all_to_all(outgoing, 'col', split_axis=0, concat_axis=0, tiled=True)]
    pallas_call x1, Pallas kernels: 90 us -> 117 us  [handover(): pl.pallas_call(functools.partial(handover_kernel, chain), in_specs=[anywh...]
    unnamed x41 -> x31, local copies, waits for them, and re-layouts: 15.7 us -> 16.2 us
  transfers between devices with their start and end apart: 2 -> 1, of which waited for: 0 -> 1; matrix products, arithmetic and copies ran while one was open for 0% -> 0% of each run, Pallas kernels for 19% -> 20%
where the time goes in v4:
time: 337 us; the launch traced here: 332 us
  Pallas kernels  215 us (64%)
  waiting for transfers between devices  66.3 us (20%)
  local copies, waits for them, and re-layouts  22.9 us (7%)
  blocking collectives  14.3 us (4%)
  starting transfers between devices  10.6 us (3%)
    pallas_call x1, Pallas kernels, handover(): pl.pallas_call(functools.partial(handover_kernel, chain), in_specs=[anywh...  117 us
    all_to_all x1, waiting for transfers between devices, local(): lax.all_to_all(outgoing, 'col', split_axis=0, concat_axis=0, tiled=True)  66.3 us
    pallas_call x1, Pallas kernels, row_gather(): pl.pallas_call(row_gather_kernel, in_specs=[pl.BlockSpec(memory_space=pl....  39.5 us
    pallas_call x1, Pallas kernels, project(): pl.pallas_call(project_kernel, grid_spec=pltpu.PrefetchScalarGridSpec(num...  30.9 us
    pallas_call x1, Pallas kernels, scan_all(): pl.pallas_call(scan_kernel, grid_spec=pltpu.PrefetchScalarGridSpec(num_sc...  19.5 us
    unnamed x31, local copies, waits for them, and re-layouts  16.2 us
    all_gather x1, blocking collectives, local(): table = lax.all_gather(page_table.reshape(pages_dev, 2), 'col', axis=0)  14.3 us
    all_to_all x1, starting transfers between devices, local(): lax.all_to_all(outgoing, 'col', split_axis=0, concat_axis=0, tiled=True)  10.6 us
  transfers between devices with their start and end apart: 1, of which 1 were waited for; matrix products, arithmetic and copies ran while one was open for 0% of the time, Pallas kernels for 20%

profile of v4, /device:TPU:12, one launch (start us, length us, event | category | flops | bytes accessed | tf_op | source)
XLA Modules:
  0.0 331.9 jit_solution(14101970121182443543)
XLA Ops:
  0.7 0.8 slice_reduce_fusion
  1.5 0.7 copy.50
  2.5 14.3 %all_gather.3 = s32[8,12,2]{1,2,0:T(2,128)S(1)} all-gather(s32[1,12,2]{1,2,0:T(2,128)S(1)} %all_gather_reshape.3), channel_id=1, replica_groups=mesh['row'=4,'col'=8] {'col'}, dimensions={0}, use_global_device_ids=true | all-gather | bytes 864 | tf_op jit(solution)/shard_map/all_gather | solution.py:548
  16.8 1.1 convert_element_type.18
  18.0 0.3 copy.57
  18.7 1.1 copy-done.1
  19.8 117.4 %handover.1 = (bf16[8,4,64,2048]{3,2,1,0:T(8,128)(2,1)}, bf16[8,64,768]{2,1,0:T(8,128)(2,1)S(1)}, bf16[8,64,256]{2,1,0:T(8,128)(2,1)S(1)}, bf16[4,1536,512]{2,1,0:T(8,128)(2,1)}) custom-call(bf16[4,64,2048]{2,1,0:T(8,128)(2,1)S(1)} %pad_maximum_fusion.in_parts, bf16[8,64,768]{2,1,0:T(8,128)(2,1)S(1)} %bitcast.40, bf16[8,64,256]{2,1,0:T(8,128)(2,1)S(1)} %bitcast.41, ...), custom_call_target="tpu_custom_call" | custom-call | bytes 300000000 | tf_op jit(solution)/shard_map/handover/pallas_call | solution.py:163
  137.3 30.9 %project.1 = (bf16[1536,512]{1,0:T(8,128)(2,1)S(1)}, bf16[1536,512]{1,0:T(8,128)(2,1)S(1)}, bf16[1536,512]{1,0:T(8,128)(2,1)S(1)}, f32[1536,128]{1,0:T(8,128)S(1)}, bf16[24,2,128,512]{3,2,1,0:T(8,128)(2,1)}) custom-call(s32[3]{0:T(128)S(1)} %copy-done.6, s32[12]{0:T(128)S(1)} %multiply_add_fusion.spots, bf16[4,1536,512]{2,1,0:T(8,128)(2,1)} %get-tuple-element.21.tok, ...), custom_call_target="tpu_custom_call" | custom-call | flops 9663676416 | bytes 30000000 | tf_op jit(solution)/shard_map/project/pallas_call | solution.py:323
  168.2 1.1 copy-done.7
  169.4 1.1 copy-done.9
  170.5 0.9 copy-done.10
  171.4 10.6 %all-to-all-start = ((bf16[24,2,128,512]{3,2,1,0:T(8,128)(2,1)}), bf16[24,2,128,512]{3,2,1,0:T(8,128)(2,1)}, u32[]{:S(2)}, u32[]{:S(2)}) async-start(bf16[24,2,128,512]{3,2,1,0:T(8,128)(2,1)} %get-tuple-element.29), calls=%async_computation | async-start | bytes 12582912 | tf_op jit(solution)/shard_map/all_to_all | solution.py:565
  182.1 0.3 convert_reduce_fusion
  182.6 1.4 copy-done.8
  184.0 1.1 copy-done.11
  185.1 19.5 %scan.1 = (bf16[1536,512]{1,0:T(8,128)(2,1)S(1)}, f32[3,4,128,128]{3,2,1,0:T(8,128)}) custom-call(s32[3]{0:T(128)S(1)} %copy-done.6, s32[3,4]{1,0:T(4,128)S(1)} %copy-done.4, bf16[1536,512]{1,0:T(8,128)(2,1)S(1)} %get-tuple-element.23.q_ref, bf16[1536,512]{1,0:T(8,128)(2,1)S(1)} %copy-done.8, bf16[1536,512]{1,0:T(8,128)(2,1)} %copy-done.9, ...), custom_call_target="tpu_custom_call" | custom-call | flops 12000000000 | bytes 5000000 | tf_op jit(solution)/shard_map/scan/pallas_call | solution.py:444
  204.6 39.5 %row_gather.1.heads_all = bf16[4,1536,512]{2,1,0:T(8,128)(2,1)} custom-call(bf16[1536,512]{1,0:T(8,128)(2,1)S(1)} %get-tuple-element.27.mine), custom_call_target="tpu_custom_call" | custom-call | bytes 100000000 | tf_op jit(solution)/shard_map/row_gather/pallas_call | solution.py:237
  244.2 0.3 select_reduce_fusion
  244.5 7.3 %out_project.1 = bf16[1536,512]{1,0:T(8,128)(2,1)} custom-call(bf16[4,1536,512]{2,1,0:T(8,128)(2,1)} %row_gather.1.heads_all, bf16[8,4,64,2048]{3,2,1,0:T(8,128)(2,1)} %get-tuple-element.22.win.wout), custom_call_target="tpu_custom_call" | custom-call | flops 3221225472 | bytes 5000000 | tf_op jit(solution)/shard_map/out_project/pallas_call | solution.py:485
  251.9 66.3 %all-to-all-done = bf16[24,2,128,512]{3,2,1,0:T(8,128)(2,1)} async-done(((bf16[24,2,128,512]{3,2,1,0:T(8,128)(2,1)}), bf16[24,2,128,512]{3,2,1,0:T(8,128)(2,1)}, u32[]{:S(2)}, u32[]{:S(2)}) %all-to-all-start) | async-done | bytes 6291488 | tf_op jit(solution)/shard_map/all_to_all | solution.py:565
  318.2 5.3 %gather_fusion = bf16[12,2,128,512]{3,2,1,0:T(8,128)(2,1)} fusion(bf16[24,2,128,512]{3,2,1,0:T(8,128)(2,1)} %all-to-all-done, s32[1024]{0:T(1024)S(1)} %pad_clamp_fusion), kind=kCustom, calls=%fused_computation | custom fusion | bytes 6291504 | tf_op jit(solution)/shard_map/jit(_take)/gather | solution.py:570
  323.5 6.8 %copy.56 = bf16[12,128,2,512]{3,2,1,0:T(2,128)(2,1)} copy(bf16[12,128,2,512]{3,1,2,0:T(8,128)(2,1)} %bitcast.45) | data formatting | bytes 6291456
  330.3 0.9 copy.72
  331.2 0.7 copy.73
  (41 shorter events, 1.2 us)
Async XLA Ops:
  0.6 17.3 %copy-start = (f32[2048,16]{0,1:T(8,128)S(1)}, f32[2048,16]{0,1:T(8,128)}, u32[]{:S(2)}) copy-start(f32[2048,16]{0,1:T(8,128)} %param.14) | copy-start | bytes 393220
  0.6 17.7 %copy-start.12 = (f32[64,6144]{1,0:T(8,128)S(1)}, f32[64,6144]{1,0:T(8,128)}, u32[]{:S(2)}) copy-start(f32[64,6144]{1,0:T(8,128)} %param.12) | copy-start | bytes 4718596
  18.4 1.4 copy-start.1
  18.5 118.8 %copy-start.2 = (bf16[3,3,1536]{2,1,0:T(4,128)(2,1)S(1)}, bf16[3,3,1536]{2,1,0:T(4,128)(2,1)}, u32[]{:S(2)}) copy-start(bf16[3,3,1536]{2,1,0:T(4,128)(2,1)} %prior.1) | copy-start | bytes 82948
  18.5 118.8 %copy-start.3 = (f32[4,1536]{1,0:T(4,128)S(1)}, f32[4,1536]{1,0:T(4,128)}, u32[]{:S(2)}) copy-start(f32[4,1536]{1,0:T(4,128)} %taps.1) | copy-start | bytes 73732
  18.6 118.8 %copy-start.6 = (s32[3]{0:T(128)S(1)}, s32[3]{0:T(128)}, u32[]{:S(2)}) copy-start(s32[3]{0:T(128)} %lens.3) | copy-start | bytes 40
  168.2 1.1 copy-start.7
  169.4 1.1 copy-start.9
  170.5 0.9 copy-start.10
  171.4 11.2 %copy-start.4 = (s32[3,4]{1,0:T(4,128)S(1)}, s32[3,4]{1,0:T(4,128)}, u32[]{:S(2)}) copy-start(s32[3,4]{1,0:T(4,128)} %picks.1) | copy-start | bytes 148
  171.4 11.2 %copy-start.5 = (f32[512]{0:T(512)S(1)}, f32[512]{0:T(512)}, u32[]{:S(2)}) copy-start(f32[512]{0:T(512)} %param.17) | copy-start | bytes 6148
  171.4 146.8 %all-to-all-start = ((bf16[24,2,128,512]{3,2,1,0:T(8,128)(2,1)}), bf16[24,2,128,512]{3,2,1,0:T(8,128)(2,1)}, u32[]{:S(2)}, u32[]{:S(2)}) async-start(bf16[24,2,128,512]{3,2,1,0:T(8,128)(2,1)} %get-tuple-element.29), calls=%async_computation | async-start | bytes 12582912 | tf_op jit(solution)/shard_map/all_to_all | solution.py:565
  182.6 1.4 copy-start.8
  184.0 1.1 copy-start.11
